TPU v7x, 512 devices: a whole 4x4x16 slice. The times are simulated.
512 devices in a mesh: ctx: 128 (over y, z, core), tp: 4 (over x).
Axes of the slice: x: 4, y: 4, z: 16, core: 2. Of those that a mesh axis runs over, the one named last changes fastest.
Arguments:
- query_raw: bfloat16 [1, 32768, 4096], P(None, 'ctx', 'tp'), may hold values from -6 to 6
- key_raw: bfloat16 [1, 32768, 4096], P(None, 'ctx', 'tp'), may hold values from -6 to 6
- value_raw: bfloat16 [1, 32768, 4096], P(None, 'ctx', 'tp'), may hold values from -6 to 6
- cotangent: bfloat16 [1, 32768, 4096], P(None, 'ctx', 'tp'), may hold values from -40 to 40
- featurizer: float32 [3, 7, 4096], P(None, None, 'tp'), may hold values from -1.6 to 1.6
- filters: bfloat16 [256, 128], P('tp'), may hold values from -0.5 to 0.5
Outputs:
- grad_query: bfloat16 [1, 32768, 4096], P(None, 'ctx', 'tp')
- grad_key: bfloat16 [1, 32768, 4096], P(None, 'ctx', 'tp')
- grad_value: bfloat16 [1, 32768, 4096], P(None, 'ctx', 'tp')
- grad_featurizer: float32 [3, 7, 4096], P(None, None, 'tp')
- grad_filters: float32 [256, 128], P('tp')
All inputs are finite; a program needn't handle non-finite values.
Results may differ from a plain program's by a relative error of at most 0.0055.
Values may be sent and summed in bfloat16 or wider, within the bound.
A program may use at most 128 MiB of HBM per device.

v0:
```python
import jax
import jax.numpy as jnp
from jax import lax
from jax.sharding import PartitionSpec as P

GROUP_SIZE = 16
FEAT_TAPS = 7
FILTER_TAPS = 128


clip_norm = 100.0


def passed_along(value, axis, steps):
    count = lax.axis_size(axis)
    leading, last = (max(0, -steps), min(count, count - steps))
    return lax.ppermute(value, axis, [(source, source + steps) for source in range(leading, last)])


def band_table(filters, lagged):
    inside = (lagged >= 0) & (lagged < FILTER_TAPS)
    picked = jnp.take(filters, jnp.clip(lagged, 0, FILTER_TAPS - 1), axis=1)
    return jnp.where(inside[None], picked, jnp.zeros_like(picked))


def causal_table(filters):
    lag_rows = jnp.arange(FILTER_TAPS)[:, None]
    lag_cols = jnp.arange(2 * FILTER_TAPS)[None, :]
    return band_table(filters, lag_rows + FILTER_TAPS - lag_cols)


def reverse_table(filters):
    lag_rows = jnp.arange(FILTER_TAPS)[:, None]
    lag_cols = jnp.arange(2 * FILTER_TAPS)[None, :]
    return band_table(filters, lag_cols - lag_rows)


def featurize(extended, weight, row_count):
    offset = extended.shape[-2] - row_count - (FEAT_TAPS - 1)
    summed = jnp.zeros(extended.shape[:-2] + (row_count, extended.shape[-1]), jnp.float32)
    for tap_index in range(FEAT_TAPS):
        first = offset + FEAT_TAPS - 1 - tap_index
        summed = summed + weight[tap_index] * extended[..., first : first + row_count, :].astype(
            jnp.float32
        )
    return summed


def adjoint(delta_ext, weight, row_count):
    summed = jnp.zeros(delta_ext.shape[:-2] + (row_count, delta_ext.shape[-1]), jnp.float32)
    for tap_index in range(FEAT_TAPS):
        summed = summed + weight[tap_index] * delta_ext[..., tap_index : tap_index + row_count, :]
    return summed


def tap_grads(delta, extended, row_count):
    offset = extended.shape[-2] - row_count - (FEAT_TAPS - 1)
    collected = []
    for tap_index in range(FEAT_TAPS):
        first = offset + FEAT_TAPS - 1 - tap_index
        piece = extended[..., first : first + row_count, :].astype(jnp.float32)
        collected.append(jnp.sum(delta * piece, axis=(0, 1)))
    return jnp.stack(collected, axis=0)


def skew_sum(moment):
    groups = moment.shape[0]
    flattened = moment.reshape(groups, 2 * FILTER_TAPS * FILTER_TAPS)
    flattened = jnp.pad(flattened, ((0, 0), (0, FILTER_TAPS)))
    skewed = flattened.reshape(groups, FILTER_TAPS, 2 * FILTER_TAPS + 1)
    return jnp.sum(skewed[:, :, 1 : FILTER_TAPS + 1], axis=1)[:, ::-1]


def to_tiles(values, groups):
    seq_count, rows, channel_count = values.shape
    shaped = values.reshape(seq_count, rows // FILTER_TAPS, FILTER_TAPS, groups, GROUP_SIZE)
    return shaped.transpose(3, 0, 1, 4, 2)


def from_tiles(tiles):
    groups, seq_count, tile_count, members, taps = tiles.shape
    return tiles.transpose(1, 2, 4, 0, 3).reshape(seq_count, tile_count * taps, groups * members)


def forward_conv(earlier, current, table):
    result = jnp.einsum(
        "gbncs,gts->gbnct", earlier, table[:, :, :FILTER_TAPS], preferred_element_type=jnp.float32
    )
    return result + jnp.einsum(
        "gbncs,gts->gbnct", current, table[:, :, FILTER_TAPS:], preferred_element_type=jnp.float32
    )


def reverse_conv(own_tiles, next_tiles, table):
    result = jnp.einsum(
        "gbnct,gst->gbncs", own_tiles, table[:, :, :FILTER_TAPS], preferred_element_type=jnp.float32
    )
    return result + jnp.einsum(
        "gbnct,gst->gbncs",
        next_tiles,
        table[:, :, FILTER_TAPS:],
        preferred_element_type=jnp.float32,
    )


def local(query_raw, key_raw, value_raw, cotangent, featurizer, filters):
    seq_count, row_count, channel_count = query_raw.shape
    groups = filters.shape[0]
    rim_rows = FILTER_TAPS + 8
    prior_query, prior_key, prior_value = passed_along(
        (query_raw[:, -rim_rows:], key_raw[:, -rim_rows:], value_raw[:, -rim_rows:]), "ctx", 1
    )
    query_ext = jnp.concatenate([prior_query, query_raw], axis=1)
    key_ext = jnp.concatenate([prior_key, key_raw], axis=1)
    value_ext = jnp.concatenate([prior_value, value_raw], axis=1)
    query_feat = featurize(query_ext, featurizer[0], row_count)
    key_long = featurize(key_ext, featurizer[1], row_count + FILTER_TAPS)
    value_long = featurize(value_ext, featurizer[2], row_count + FILTER_TAPS)
    product_ext = (key_long * value_long).astype(jnp.bfloat16)
    key_feat = key_long[:, FILTER_TAPS:]
    value_feat = value_long[:, FILTER_TAPS:]
    product_tiles = to_tiles(product_ext, groups)
    earlier = product_tiles[:, :, :-1]
    current = product_tiles[:, :, 1:]
    forward_table = causal_table(filters)
    convolved = from_tiles(forward_conv(earlier, current, forward_table))
    upstream = cotangent.astype(jnp.float32)
    mid_grad = (upstream * query_feat).astype(jnp.bfloat16)
    query_delta = upstream * convolved
    mid_tiles = to_tiles(mid_grad, groups)
    backward_table = reverse_table(filters)
    after_mid = passed_along(mid_grad[:, :FILTER_TAPS], "ctx", -1)
    following = to_tiles(jnp.concatenate([mid_grad[:, FILTER_TAPS:], after_mid], axis=1), groups)
    product_grad = from_tiles(reverse_conv(mid_tiles, following, backward_table))
    key_delta = product_grad * value_feat
    value_delta = product_grad * key_feat
    after_query, after_key, after_value = (
        passed_along(query_delta[:, :8].astype(jnp.bfloat16), "ctx", -1).astype(jnp.float32),
        passed_along(key_delta[:, :8].astype(jnp.bfloat16), "ctx", -1).astype(jnp.float32),
        passed_along(value_delta[:, :8].astype(jnp.bfloat16), "ctx", -1).astype(jnp.float32),
    )
    grad_query = adjoint(
        jnp.concatenate([query_delta, after_query], axis=1), featurizer[0], row_count
    ).astype(jnp.bfloat16)
    grad_key = adjoint(
        jnp.concatenate([key_delta, after_key], axis=1), featurizer[1], row_count
    ).astype(jnp.bfloat16)
    grad_value = adjoint(
        jnp.concatenate([value_delta, after_value], axis=1), featurizer[2], row_count
    ).astype(jnp.bfloat16)
    feat_grad = jnp.stack(
        [
            tap_grads(query_delta, query_ext, row_count),
            tap_grads(key_delta, key_ext, row_count),
            tap_grads(value_delta, value_ext, row_count),
        ],
        axis=0,
    )
    moment_early = jnp.einsum(
        "gbnct,gbncs->gts", mid_tiles, earlier, preferred_element_type=jnp.float32
    )
    moment_now = jnp.einsum(
        "gbnct,gbncs->gts", mid_tiles, current, preferred_element_type=jnp.float32
    )
    filter_grad = skew_sum(jnp.concatenate([moment_early, moment_now], axis=2))
    feat_total, filter_total = lax.psum((feat_grad, filter_grad), "ctx")
    local_square = jnp.sum(feat_total * feat_total) + jnp.sum(filter_total * filter_total)
    squared = lax.psum(local_square, "tp")
    factor = 1.0 / jnp.maximum(1.0, jnp.sqrt(squared) / clip_norm)
    return (grad_query, grad_key, grad_value, factor * feat_total, factor * filter_total)


def solution(mesh):
    return jax.shard_map(
        local,
        mesh=mesh,
        in_specs=(
            P(None, "ctx", "tp"),
            P(None, "ctx", "tp"),
            P(None, "ctx", "tp"),
            P(None, "ctx", "tp"),
            P(None, None, "tp"),
            P("tp", None),
        ),
        out_specs=(
            P(None, "ctx", "tp"),
            P(None, "ctx", "tp"),
            P(None, "ctx", "tp"),
            P(None, None, "tp"),
            P("tp", None),
        ),
        check_vma=False,
    )
```

profile of v0, /device:TPU:1, one launch (start us, length us, event | category | flops | bytes accessed | tf_op | source)
XLA Modules:
  0.0 1207.2 jit_solution(13227124777677333385)
XLA Ops:
  7.2 1.0 slice.390
  8.2 4.9 collective-permute-start.3
  13.1 1.0 slice.359
  14.1 1.9 collective-permute-start.1
  16.1 1.0 slice.344
  17.0 3.9 collective-permute-start
  21.0 0.1 fusion.88
  21.1 0.2 fusion.93
  21.3 0.1 fusion.92
  21.4 0.1 copy.94
  21.5 0.1 copy.118
  21.6 114.1 %gather_fusion = bf16[32768,64]{1,0:T(8,128)(2,1)} fusion(bf16[64,128]{0,1:T(8,128)(2,1)S(1)} %copy.94, s32[32768]{0:T(1024)S(1)} %broadcast_clamp_fusion.1), kind=kCustom, calls=%fused_computation.clone | custom fusion | bytes 8519680 | tf_op jit(solution)/shard_map/jit(_take)/gather | solution.py:22
  135.8 10.1 copy.116
  145.9 0.1 copy.119
  146.0 114.2 %gather_fusion.1 = bf16[32768,64]{1,0:T(8,128)(2,1)} fusion(bf16[64,128]{0,1:T(8,128)(2,1)S(1)} %copy.94, s32[32768]{0:T(1024)S(1)} %broadcast_clamp_fusion), kind=kCustom, calls=%fused_computation.1.clone | custom fusion | bytes 8519680 | tf_op jit(solution)/shard_map/jit(_take)/gather | solution.py:22
  260.1 10.1 copy.117
  270.2 4.8 bitcast_select_fusion.1
  275.1 2.5 bitcast_select_fusion
  277.8 0.9 copy-done.15
  278.6 1.0 fusion.8
  279.7 1.0 copy.98
  280.7 0.8 fusion.95
  281.6 4.1 multiply_convert_fusion
  285.7 1.2 copy.92
  286.9 3.3 reshape.212
  290.2 1.4 copy.133
  291.5 2.0 reshape.216
  293.5 3.8 convolution_bitcast_fusion
  297.3 2.7 convolution_bitcast_fusion.1
  300.1 0.6 copy-done.1
  300.7 1.2 fusion.2
  301.9 1.2 fusion.5
  303.1 1.6 copy.96
  304.7 3.7 copy.97
  308.4 3.0 fusion.21
  311.5 2.1 collective-permute-start.2
  313.6 1.9 collective-permute-start.4
  315.5 6.2 pad_maximum_fusion
  321.7 9.2 copy.120
  330.9 7.2 pad.4
  338.1 14.2 %reshape.222 = f32[64,128,257]{2,1,0:T(8,128)} reshape(f32[64,32896]{1,0:T(8,128)} %pad.4) | data formatting | bytes 16842752 | tf_op jit(solution)/shard_map/reshape | solution.py:70
  352.3 4.7 slice_reduce_fusion
  357.0 0.1 rev.3
  357.1 495.4 %psum.22 = f32[64,128]{1,0:T(8,128)S(1)} all-reduce(f32[64,128]{1,0:T(8,128)S(1)} %rev.3), channel_id=1, replica_groups=mesh['ctx'=128,'tp'=4] {'ctx'}, use_global_device_ids=true, to_apply=%region_24.26 | all-reduce | flops 8192 | bytes 65536 | tf_op jit(solution)/shard_map/psum | solution.py:166
  852.5 0.7 multiply_reduce_fusion.15
  853.3 1.7 fusion.60
  855.0 0.2 copy.102
  855.2 0.1 reshape.218
  855.4 2.8 fusion
  858.2 2.8 fusion.7
  861.0 1.5 copy.104
  862.6 3.7 copy.105
  866.3 3.5 multiply_reduce_fusion
  869.8 1.0 copy-done.10
  870.8 7.5 collective-permute-start.5
  878.4 2.1 collective-permute-start.6
  880.6 0.7 pad_maximum_fusion.5
  881.3 6.3 fusion.43
  887.6 297.3 %all-reduce.3.cloned.1.call-done = f32[3,7,1024]{2,1,0:T(8,128)} async-done(((f32[3,7,1024]{2,1,0:T(8,128)}), f32[3,7,1024]{2,1,0:T(8,128)}) %all-reduce.3.cloned.1.call-update) | async-done | bytes 86032 | tf_op jit(solution)/shard_map/psum | solution.py:166
  1184.9 1.6 multiply_reduce_fusion.14
  1187.8 1.7 fusion.26
  1189.4 8.9 psum.23
  1199.0 0.6 broadcast_multiply_fusion.1
  1199.7 0.6 broadcast_multiply_fusion
  (78 shorter events, 0.7 us)
Async XLA Ops:
  7.2 14.2 %copy-start.20 = (bf16[64,128]{1,0:T(8,128)(2,1)S(1)}, bf16[64,128]{1,0:T(8,128)(2,1)}, u32[]{:S(2)}) copy-start(bf16[64,128]{1,0:T(8,128)(2,1)} %param.13) | copy-start | bytes 49156
  7.2 1177.7 %all-reduce.3.cloned.1.call-start = ((), (), s32[]{:S(2)}) async-start(), calls=%async_computation | async-start | bytes 196608 | tf_op jit(solution)/shard_map/psum | solution.py:166
  8.2 269.5 %collective-permute-start.3 = (bf16[1,136,1024]{2,1,0:T(8,128)(2,1)S(1)}, bf16[1,136,1024]{2,1,0:T(8,128)(2,1)S(1)}, u32[]{:S(2)}, u32[]{:S(2)}) collective-permute-start(bf16[1,136,1024]{2,1,0:T(8,128)(2,1)S(1)} %slice.390), channel_id=1, source_target_pairs={{0,4},{4,8},{8,12},{12,16},{16,20},{20,24},{24,28},{28,32},{32,36}... | collective-permute-start | bytes 835592 | tf_op jit(solution)/shard_map/ppermute | solution.py:17
  14.1 265.5 %collective-permute-start.1 = (bf16[1,136,1024]{2,1,0:T(8,128)(2,1)S(1)}, bf16[1,136,1024]{2,1,0:T(8,128)(2,1)S(1)}, u32[]{:S(2)}, u32[]{:S(2)}) collective-permute-start(bf16[1,136,1024]{2,1,0:T(8,128)(2,1)S(1)} %slice.359), channel_id=1, source_target_pairs={{0,4},{4,8},{8,12},{12,16},{16,20},{20,24},{24,28},{28,32},{32,36}... | collective-permute-start | bytes 835592 | tf_op jit(solution)/shard_map/ppermute | solution.py:17
  17.0 264.5 %collective-permute-start = (bf16[1,136,1024]{2,1,0:T(8,128)(2,1)S(1)}, bf16[1,136,1024]{2,1,0:T(8,128)(2,1)S(1)}, u32[]{:S(2)}, u32[]{:S(2)}) collective-permute-start(bf16[1,136,1024]{2,1,0:T(8,128)(2,1)S(1)} %slice.344), channel_id=1, source_target_pairs={{0,4},{4,8},{8,12},{12,16},{16,20},{20,24},{24,28},{28,32},{32,36}... | collective-permute-start | bytes 835592 | tf_op jit(solution)/shard_map/ppermute | solution.py:17
  270.2 4.9 copy-start
  275.1 2.5 copy-start.19
  275.1 2.6 copy-start.5
  277.6 1.0 copy-start.15
  278.6 1.1 copy-start.13
  279.7 1.9 copy-start.14
  293.5 3.8 copy-start.3
  297.3 3.4 copy-start.1
  304.7 3.7 copy-start.6
  304.7 3.7 copy-start.16
  308.4 7.1 copy-start.2
  311.5 10.2 copy-start.8
  311.5 541.8 %collective-permute-start.2 = (bf16[1,8,1024]{2,1,0:T(8,128)(2,1)S(1)}, bf16[1,8,1024]{2,1,0:T(8,128)(2,1)S(1)}, u32[]{:S(2)}, u32[]{:S(2)}) collective-permute-start(bf16[1,8,1024]{2,1,0:T(8,128)(2,1)S(1)} %slice.752), channel_id=1, source_target_pairs={{4,0},{8,4},{12,8},{16,12},{20,16},{24,20},{28,24},{32,28},{36,32}... | collective-permute-start | bytes 49160 | tf_op jit(solution)/shard_map/ppermute | solution.py:17
  313.6 541.4 %collective-permute-start.4 = (bf16[1,128,1024]{2,1,0:T(8,128)(2,1)}, bf16[1,128,1024]{2,1,0:T(8,128)(2,1)S(1)}, u32[]{:S(2)}, u32[]{:S(2)}) collective-permute-start(bf16[1,128,1024]{2,1,0:T(8,128)(2,1)} %get-tuple-element.52), channel_id=1, source_target_pairs={{4,0},{8,4},{12,8},{16,12},{20,16},{24,20},{28,24},{32,28},{36,32}... | collective-permute-start | bytes 786440 | tf_op jit(solution)/shard_map/ppermute | solution.py:17
  352.3 500.9 %copy-start.21 = (f32[1024]{0:T(1024)S(1)}, f32[1024]{0:T(1024)}, u32[]{:S(2)}) copy-start(f32[1024]{0:T(1024)} %get-tuple-element.19) | copy-start | bytes 12292
  352.3 500.9 %copy-start.22 = (f32[1024]{0:T(1024)S(1)}, f32[1024]{0:T(1024)}, u32[]{:S(2)}) copy-start(f32[1024]{0:T(1024)} %get-tuple-element.20) | copy-start | bytes 12292
  352.3 500.9 %copy-start.23 = (f32[1024]{0:T(1024)S(1)}, f32[1024]{0:T(1024)}, u32[]{:S(2)}) copy-start(f32[1024]{0:T(1024)} %get-tuple-element.21) | copy-start | bytes 12292
  352.3 500.9 %copy-start.24 = (f32[1024]{0:T(1024)S(1)}, f32[1024]{0:T(1024)}, u32[]{:S(2)}) copy-start(f32[1024]{0:T(1024)} %get-tuple-element.34) | copy-start | bytes 12292
  352.3 501.0 %copy-start.9 = (f32[1,256,1024]{2,1,0:T(8,128)S(1)}, f32[1,256,1024]{2,1,0:T(8,128)}, u32[]{:S(2)}) copy-start(f32[1,256,1024]{2,1,0:T(8,128)} %copy-done.8) | copy-start | bytes 3145732
  357.0 498.0 %copy-start.17 = (bf16[1,128,1024]{2,1,0:T(8,128)(2,1)S(1)}, bf16[1,128,1024]{2,1,0:T(8,128)(2,1)}, u32[]{:S(2)}) copy-start(bf16[1,128,1024]{2,1,0:T(8,128)(2,1)} %get-tuple-element.51) | copy-start | bytes 786436
  855.4 2.9 copy-start.4
  862.6 3.7 copy-start.7
  869.8 1.0 copy-start.10
  869.8 8.6 copy-start.11
  870.8 10.4 collective-permute-start.5
  878.4 309.3 %copy-start.12 = (f32[1,256,1024]{2,1,0:T(8,128)S(1)}, f32[1,256,1024]{2,1,0:T(8,128)}, u32[]{:S(2)}) copy-start(f32[1,256,1024]{2,1,0:T(8,128)} %copy-done.11) | copy-start | bytes 3145732
  878.4 9.2 collective-permute-start.6
  1184.9 14.8 %copy-start.18 = (f32[3,7,1024]{2,1,0:T(8,128)S(1)}, f32[3,7,1024]{2,1,0:T(8,128)}, u32[]{:S(2)}) copy-start(f32[3,7,1024]{2,1,0:T(8,128)} %all-reduce.3.cloned.1.call-done) | copy-start | bytes 258052
Sparse Core Ops, SparseCore 0:
  881.4 303.4 all-reduce.2
where the time goes:
time: 1210 us
  blocking collectives  504 us (42%)
  local copies, waits for them, and re-layouts  306 us (25%)
  waiting for transfers between devices  297 us (25%)
  other arithmetic  44.2 us (4%)
  starting transfers between devices  24.4 us (2%)
  between operations  16.5 us (1%)
  matrix products  14.6 us (1%)
    psum x1, blocking collectives, local(): feat_total, filter_total = lax.psum((feat_grad, filter_grad), 'ctx')  495 us
    psum x1, waiting for transfers between devices, local(): feat_total, filter_total = lax.psum((feat_grad, filter_grad), 'ctx')  297 us
    gather x4, local copies, waits for them, and re-layouts, band_table(): picked = jnp.take(filters, jnp.clip(lagged, 0, FILTER_TAPS - 1), axis=1)  249 us
    ppermute x7, starting transfers between devices, passed_along(): lax.ppermute(value, axis, [(source, source + steps) for source in range(l...  24.4 us
  transfers between devices with their start and end apart: 8, of which 1 were waited for; matrix products, arithmetic and copies ran while one was open for 26% of the time, Pallas kernels for 0%

commit v1 on v0

v1 whole, which is shorter than its diff:
```python
import jax
import jax.numpy as jnp
from jax import lax
from jax.experimental import pallas as pl
from jax.experimental.pallas import tpu as pltpu
from jax.sharding import PartitionSpec as P

GROUP = 16
TAPS = 7
LAGS = 128
LANES = 128
HALO = 16
BLOCK = 16
WIN = LAGS + BLOCK
CLIP = 100.0
F32 = jnp.float32
BF16 = jnp.bfloat16
MESH = pl.DeviceIdType.MESH
NY, NZ, NX = 4, 16, 4


def remote(src, dst, send, recv, device):
    return pltpu.make_async_remote_copy(
        src_ref=src, dst_ref=dst, send_sem=send, recv_sem=recv, device_id=device, device_id_type=MESH
    )


def kernel(
    q_ref,
    k_ref,
    v_ref,
    cot_ref,
    feat_ref,
    filt_ref,
    gq_ref,
    gk_ref,
    gv_ref,
    gfeat_ref,
    gfilt_ref,
    halo,
    raw,
    kfeat,
    vfeat,
    prod,
    mid,
    delta,
    tabs,
    fwd_tab,
    rev_tab,
    moment,
    pay,
    got1,
    got2,
    part,
    got3,
    full3,
    full,
    norms,
    norm2,
    s_halo,
    r_halo,
    s_big,
    r_big,
    s_del,
    r_del,
    s_core,
    r_core,
    s_y,
    r_y,
    s_z,
    r_z,
    s_xy,
    r_xy,
):
    rows, channels = q_ref.shape
    cols = channels // LANES
    per_col = LANES // GROUP
    groups = filt_ref.shape[0]
    half = rows // 2
    ctx = lax.axis_index("ctx")
    tp = lax.axis_index("tp")
    n_ctx = 2 * NY * NZ
    core = lax.rem(ctx, 2)
    zi = lax.rem(lax.div(ctx, 2), NZ)
    yi = lax.div(ctx, 2 * NZ)

    def at(x, y, z, c):
        return ((y * NZ + z) * 2 + c, x)

    first = ctx == 0
    last = ctx == n_ctx - 1
    after = (lax.rem(ctx + 1, n_ctx), tp)
    before = (lax.rem(ctx + n_ctx - 1, n_ctx), tp)
    twin = at(tp, yi, zi, 1 - core)
    z_peers = [at(tp, yi, lax.rem(zi + d, NZ), core) for d in range(1, NZ)]
    y_peers = [at(tp, lax.rem(yi + d, NY), zi, core) for d in range(1, NY)]
    xy_peers = [
        at(lax.rem(tp + dx, NX), lax.rem(yi + dy, NY), zi, core)
        for dx in range(NX)
        for dy in range(NY)
        if dx or dy
    ]

    barrier = pltpu.get_barrier_semaphore()
    greeted = [after, before] + z_peers + xy_peers
    for peer in greeted:
        pl.semaphore_signal(barrier, inc=1, device_id=peer, device_id_type=MESH)

    moment[2, pl.ds(0, 8), :] = jnp.zeros((8, LANES), F32)

    lag_row = lax.broadcasted_iota(jnp.int32, (LAGS, 2 * LANES), 0)
    lag_col = lax.broadcasted_iota(jnp.int32, (LAGS, 2 * LANES), 1)
    flip = jnp.where(lag_row + lag_col == LAGS, 1.0, 0.0).astype(BF16)
    keep = jnp.where(lag_row == lag_col, 1.0, 0.0).astype(BF16)
    for pick, table in ((flip, fwd_tab), (keep, rev_tab)):
        wide = jnp.dot(filt_ref[...], pick, preferred_element_type=F32)
        for b in range(BLOCK):
            moved = pltpu.roll(wide, b, 1) if b else wide
            tabs[0, pl.ds(b, groups, stride=BLOCK), :] = moved[:, :LANES]
            tabs[1, pl.ds(b, groups, stride=BLOCK), :] = moved[:, LANES:]
        for j in range(cols):
            span = pl.ds(j * LANES, LANES)
            table[j] = jnp.concatenate([tabs[0, span, :], tabs[1, span, :]], axis=1).astype(BF16)

    pl.semaphore_wait(barrier, len(greeted))

    halo_copies = [
        remote(ref.at[pl.ds(rows - HALO, HALO), :], halo.at[s], s_halo.at[s], r_halo.at[s], after)
        for s, ref in enumerate((q_ref, k_ref, v_ref))
    ]
    for copy in halo_copies:
        copy.start()

    def lanes_of(j):
        return pl.ds(pl.multiple_of(j * LANES, LANES), LANES)

    def weights(s, j):
        return [feat_ref[s, pl.ds(tap, 1), lanes_of(j)] for tap in range(TAPS)]

    def featurized(s, j, taps, start, count):
        total = taps[0] * raw[s, j, pl.ds(HALO + start, count), :]
        for tap in range(1, TAPS):
            total = total + taps[tap] * raw[s, j, pl.ds(HALO + start - tap, count), :]
        return total

    chunk = 64

    def products(j, starts):
        k_taps, v_taps = weights(1, j), weights(2, j)
        for start in starts:
            here = pl.ds(start, chunk)
            k_here = featurized(1, j, k_taps, start, chunk)
            v_here = featurized(2, j, v_taps, start, chunk)
            kfeat[j, here, :] = k_here
            vfeat[j, here, :] = v_here
            prod[j, pl.ds(LAGS + start, chunk), :] = (k_here * v_here).astype(BF16)

    def mids(j, starts):
        q_taps = weights(0, j)
        for start in starts:
            here = pl.ds(start, chunk)
            q_here = featurized(0, j, q_taps, start, chunk)
            upstream = cot_ref[here, lanes_of(j)].astype(F32)
            mid[j, here, :] = (upstream * q_here).astype(BF16)

    @pl.loop(0, cols)
    def _(j):
        for s, ref in enumerate((q_ref, k_ref, v_ref)):
            raw[s, j, pl.ds(HALO, rows), :] = ref[:, lanes_of(j)].astype(F32)
        products(j, range(half, rows, chunk))

    send_prod = remote(
        prod.at[:, pl.ds(rows, LAGS), :], prod.at[:, pl.ds(0, LAGS), :], s_big.at[0], r_big.at[0], after
    )
    send_prod.start()

    for copy in halo_copies:
        copy.wait_recv()

    @pl.loop(0, cols)
    def _(j):
        for s in range(3):
            got = halo[s, :, lanes_of(j)].astype(F32)
            raw[s, j, pl.ds(0, HALO), :] = jnp.where(first, 0.0, got)
        mids(j, range(0, half, chunk))

    send_mid = remote(
        mid.at[:, pl.ds(0, LAGS), :], mid.at[:, pl.ds(rows, LAGS), :], s_big.at[1], r_big.at[1], before
    )
    send_mid.start()

    @pl.loop(0, cols)
    def _(j):
        mids(j, range(half, rows, chunk))
        products(j, range(0, half, chunk))

    lane_group = lax.broadcasted_iota(jnp.int32, (BLOCK, LANES), 1) // GROUP

    def picked(stacked, lane0):
        out = stacked[0:BLOCK, lane0 : lane0 + LANES]
        for g in range(1, per_col):
            piece = stacked[g * BLOCK : (g + 1) * BLOCK, lane0 : lane0 + LANES]
            out = jnp.where(lane_group == g, piece, out)
        return out

    def window(ref, j, a):
        near = ref[j, pl.ds(a * BLOCK, WIN), :]
        far = ref[j, pl.ds(a * BLOCK + half, WIN), :]
        return jnp.concatenate([near, far], axis=1)

    def tap_sums(j, s, acc, d, start, count):
        out = []
        for tap in range(TAPS):
            moved = raw[s, j, pl.ds(HALO + start - tap, count), :]
            term = jnp.sum((d * moved).reshape(count // 8, 8, LANES), axis=0)
            out.append(term if acc is None else acc[tap] + term)
        return out

    send_prod.wait_recv()

    @pl.when(first)
    def _():
        prod[:, pl.ds(0, LAGS), :] = jnp.zeros((cols, LAGS, LANES), BF16)

    @pl.loop(0, cols)
    def _(j):
        band = fwd_tab[j][:, :WIN]
        acc = None
        for a in range(half // BLOCK):
            stacked = jnp.dot(band, window(prod, j, a), preferred_element_type=F32)
            for side in range(2):
                start = a * BLOCK + side * half
                upstream = cot_ref[pl.ds(start, BLOCK), lanes_of(j)].astype(F32)
                d = upstream * picked(stacked, side * LANES)
                delta[0, j, pl.ds(start, BLOCK), :] = d
                acc = tap_sums(j, 0, acc, d, start, BLOCK)
        for tap in range(TAPS):
            moment[2, pl.ds(tap, 1), :] = jnp.sum(acc[tap], axis=0, keepdims=True)
        pay[j, pl.ds(0, 8), :] = moment[2, pl.ds(0, 8), :]

    send_mid.wait_recv()

    @pl.when(last)
    def _():
        mid[:, pl.ds(rows, LAGS), :] = jnp.zeros((cols, LAGS, LANES), BF16)

    row_group = lax.broadcasted_iota(jnp.int32, (LANES, 2 * LANES), 0) // BLOCK
    col_group = lax.rem(lax.broadcasted_iota(jnp.int32, (LANES, 2 * LANES), 1), LANES) // GROUP
    own = jnp.where(row_group == col_group, 1.0, 0.0).astype(BF16)

    @pl.loop(0, cols)
    def _(j):
        band = rev_tab[j][:, :WIN]
        acc_k = None
        acc_v = None
        pairs = jnp.zeros((LANES, WIN), F32)
        for a in range(half // BLOCK):
            ahead = window(mid, j, a)
            stacked = jnp.dot(band, ahead, preferred_element_type=F32)
            for side in range(2):
                start = a * BLOCK + side * half
                here = pl.ds(start, BLOCK)
                pg = picked(stacked, side * LANES)
                dk = pg * vfeat[j, here, :]
                dv = pg * kfeat[j, here, :]
                delta[1, j, here, :] = dk
                delta[2, j, here, :] = dv
                acc_k = tap_sums(j, 1, acc_k, dk, start, BLOCK)
                acc_v = tap_sums(j, 2, acc_v, dv, start, BLOCK)
            base = jnp.concatenate(
                [
                    prod[j, pl.ds(LAGS + a * BLOCK, BLOCK), :],
                    prod[j, pl.ds(LAGS + a * BLOCK + half, BLOCK), :],
                ],
                axis=1,
            )
            spread = jnp.concatenate([base] * per_col, axis=0) * own
            pairs = pairs + lax.dot_general(
                spread, ahead, (((1,), (1,)), ((), ())), preferred_element_type=F32
            )
        for s, acc in ((1, acc_k), (2, acc_v)):
            for tap in range(TAPS):
                moment[2, pl.ds(tap, 1), :] = jnp.sum(acc[tap], axis=0, keepdims=True)
            pay[j, pl.ds(s * 8, 8), :] = moment[2, pl.ds(0, 8), :]
        moment[0] = pairs[:, :LANES]
        moment[1, :, pl.ds(0, BLOCK)] = pairs[:, LANES:]
        lags = moment[0, pl.ds(0, per_col, stride=BLOCK), :]
        for b in range(1, BLOCK):
            low = moment[0, pl.ds(b, per_col, stride=BLOCK), :]
            high = moment[1, pl.ds(b, per_col, stride=BLOCK), :]
            both = pltpu.roll(jnp.concatenate([low, high], axis=1), 2 * LANES - b, 1)
            lags = lags + both[:, :LANES]
        pay[j, pl.ds(24, per_col), :] = lags

    send_del = remote(
        delta.at[:, :, pl.ds(0, 8), :], delta.at[:, :, pl.ds(rows, 8), :], s_del.at[0], r_del.at[0], before
    )
    send_del.start()

    pieces = 2 * NY
    per_core = cols // 2
    core1 = remote(
        pay.at[pl.ds((1 - core) * per_core, per_core)], got1, s_core.at[0], r_core.at[0], twin
    )
    core1.start()

    def adjoint(s, out_ref):
        @pl.loop(0, cols)
        def _(j):
            taps = weights(s, j)
            for start in range(0, rows, chunk):
                total = taps[0] * delta[s, j, pl.ds(start, chunk), :]
                for tap in range(1, TAPS):
                    total = total + taps[tap] * delta[s, j, pl.ds(start + tap, chunk), :]
                out_ref[pl.ds(start, chunk), lanes_of(j)] = total.astype(BF16)

    send_del.wait_recv()

    @pl.when(last)
    def _():
        delta[:, :, pl.ds(rows, 8), :] = jnp.zeros((3, cols, 8, LANES), F32)

    adjoint(0, gq_ref)

    core1.wait_recv()
    got1[...] = got1[...] + pay[pl.ds(core * per_core, per_core)]
    y_rs = [
        remote(got1.at[lax.rem(yi + d, NY)], got2.at[d - 1], s_y.at[d - 1], r_y.at[d - 1], y_peers[d - 1])
        for d in range(1, NY)
    ]
    for copy in y_rs:
        copy.start()

    adjoint(1, gk_ref)

    for copy in y_rs:
        copy.wait_recv()
    mine = got1[yi]
    for d in range(NY - 1):
        mine = mine + got2[d]
    for r in range(2 * NZ):
        part[r // 2, pl.ds(r % 2, 1), :] = mine[r : r + 1, :]
    z_rs = [
        remote(part.at[lax.rem(zi + d, NZ)], got3.at[d - 1], s_z.at[d - 1], r_z.at[d - 1], z_peers[d - 1])
        for d in range(1, NZ)
    ]
    for copy in z_rs:
        copy.start()

    adjoint(2, gv_ref)

    for copy in z_rs:
        copy.wait_recv()
    piece = part[zi]
    for d in range(NZ - 1):
        piece = piece + got3[d]
    full3[zi] = piece

    z_ag = [
        remote(full3.at[zi], full3.at[zi], s_z.at[NZ - 1 + d - 1], r_z.at[NZ - 1 + d - 1], z_peers[d - 1])
        for d in range(1, NZ)
    ]
    for copy in z_ag:
        copy.start()
    for d in range(1, NZ):
        src = lax.rem(zi + NZ - d, NZ)
        remote(
            full3.at[src], full3.at[src], s_z.at[NZ - 1 + d - 1], r_z.at[NZ - 1 + d - 1], z_peers[d - 1]
        ).wait_recv()
    slot = core * NY + yi
    for r in range(2 * NZ):
        full[slot, pl.ds(r, 1), :] = full3[r // 2, pl.ds(r % 2, 1), :]
    whole = full[slot]
    squares = jnp.sum(jnp.sum(whole * whole, axis=0, keepdims=True), axis=1, keepdims=True)
    norms[tp * NY + yi] = jnp.broadcast_to(squares, (8, LANES))
    y_ag = [
        remote(full.at[slot], full.at[slot], s_y.at[NY - 1 + d - 1], r_y.at[NY - 1 + d - 1], y_peers[d - 1])
        for d in range(1, NY)
    ]
    for copy in y_ag:
        copy.start()
    seat = tp * NY + yi
    xy_ag = [
        remote(norms.at[seat], norms.at[seat], s_xy.at[i], r_xy.at[i], peer)
        for i, peer in enumerate(xy_peers)
    ]
    for copy in xy_ag:
        copy.start()
    for d in range(1, NY):
        src = core * NY + lax.rem(yi + NY - d, NY)
        remote(
            full.at[src], full.at[src], s_y.at[NY - 1 + d - 1], r_y.at[NY - 1 + d - 1], y_peers[d - 1]
        ).wait_recv()
    i = 0
    for dx in range(NX):
        for dy in range(NY):
            if dx or dy:
                src = lax.rem(tp + NX - dx, NX) * NY + lax.rem(yi + NY - dy, NY)
                remote(norms.at[src], norms.at[src], s_xy.at[i], r_xy.at[i], xy_peers[i]).wait_recv()
                i += 1
    total = norms[0]
    for i in range(1, NX * NY):
        total = total + norms[i]
    norm2[core] = total
    core2 = remote(
        full.at[pl.ds(core * NY, NY)], full.at[pl.ds(core * NY, NY)], s_core.at[1], r_core.at[1], twin
    )
    core3 = remote(norm2.at[core], norm2.at[core], s_core.at[2], r_core.at[2], twin)
    core2.start()
    core3.start()
    remote(
        full.at[pl.ds((1 - core) * NY, NY)],
        full.at[pl.ds((1 - core) * NY, NY)],
        s_core.at[1],
        r_core.at[1],
        twin,
    ).wait_recv()
    remote(norm2.at[1 - core], norm2.at[1 - core], s_core.at[2], r_core.at[2], twin).wait_recv()
    norm = jnp.sqrt(norm2[0] + norm2[1])
    scale = (1.0 / jnp.maximum(1.0, norm / CLIP))[0:1, :]
    for j in range(cols):
        for s in range(3):
            gfeat_ref[s, :, pl.ds(j * LANES, LANES)] = scale * full[j, pl.ds(s * 8, TAPS), :]
        gfilt_ref[pl.ds(j * per_col, per_col), :] = scale * full[j, pl.ds(24, per_col), :]

    for copy in halo_copies + [send_prod, send_mid, send_del, core1, core2, core3] + y_rs + z_rs + z_ag + y_ag + xy_ag:
        copy.wait_send()


def local(query_raw, key_raw, value_raw, cotangent, featurizer, filters):
    _, rows, channels = query_raw.shape
    groups = filters.shape[0]
    cols = channels // LANES
    flat = lambda x: x.reshape(rows, channels)
    vmem = pl.BlockSpec(memory_space=pltpu.VMEM)
    grad = jax.ShapeDtypeStruct((rows, channels), BF16)
    dma = pltpu.SemaphoreType.DMA
    pay_rows = 24 + LANES // GROUP
    outs = pl.pallas_call(
        kernel,
        out_shape=(
            grad,
            grad,
            grad,
            jax.ShapeDtypeStruct(featurizer.shape, F32),
            jax.ShapeDtypeStruct(filters.shape, F32),
        ),
        in_specs=[vmem] * 6,
        out_specs=(vmem,) * 5,
        scratch_shapes=[
            pltpu.VMEM((3, HALO, channels), BF16),
            pltpu.VMEM((3, cols, HALO + rows, LANES), F32),
            pltpu.VMEM((cols, rows, LANES), F32),
            pltpu.VMEM((cols, rows, LANES), F32),
            pltpu.VMEM((cols, LAGS + rows, LANES), BF16),
            pltpu.VMEM((cols, LAGS + rows, LANES), BF16),
            pltpu.VMEM((3, cols, rows + 8, LANES), F32),
            pltpu.VMEM((2, groups * BLOCK, LANES), F32),
            pltpu.VMEM((cols, LANES, 2 * LANES), BF16),
            pltpu.VMEM((cols, LANES, 2 * LANES), BF16),
            pltpu.VMEM((3, LANES, LANES), F32),
            pltpu.VMEM((cols, pay_rows, LANES), F32),
            pltpu.VMEM((cols // 2, pay_rows, LANES), F32),
            pltpu.VMEM((NY - 1, pay_rows, LANES), F32),
            pltpu.VMEM((NZ, 2, LANES), F32),
            pltpu.VMEM((NZ - 1, 2, LANES), F32),
            pltpu.VMEM((NZ, 2, LANES), F32),
            pltpu.VMEM((cols, pay_rows, LANES), F32),
            pltpu.VMEM((NX * NY, 8, LANES), F32),
            pltpu.VMEM((2, 8, LANES), F32),
            dma((3,)),
            dma((3,)),
            dma((2,)),
            dma((2,)),
            dma((1,)),
            dma((1,)),
            dma((3,)),
            dma((3,)),
            dma((2 * (NY - 1),)),
            dma((2 * (NY - 1),)),
            dma((2 * (NZ - 1),)),
            dma((2 * (NZ - 1),)),
            dma((NX * NY - 1,)),
            dma((NX * NY - 1,)),
        ],
        compiler_params=pltpu.CompilerParams(
            collective_id=0, has_side_effects=True, vmem_limit_bytes=48 * 1024 * 1024
        ),
        cost_estimate=pl.CostEstimate(
            flops=12 * 256 * rows * channels, bytes_accessed=14 * rows * channels, transcendentals=0
        ),
    )(flat(query_raw), flat(key_raw), flat(value_raw), flat(cotangent), featurizer, filters)
    shape = query_raw.shape
    return (outs[0].reshape(shape), outs[1].reshape(shape), outs[2].reshape(shape), outs[3], outs[4])


def solution(mesh):
    stream = P(None, "ctx", "tp")
    return jax.shard_map(
        local,
        mesh=mesh,
        in_specs=(stream, stream, stream, stream, P(None, None, "tp"), P("tp", None)),
        out_specs=(stream, stream, stream, P(None, None, "tp"), P("tp", None)),
        check_vma=False,
    )
```

time: 1210 us -> 69.2 us (0.06)
  blocking collectives: 504 us -> 0 us
  waiting for transfers between devices: 297 us -> 0 us
  local copies, waits for them, and re-layouts: 306 us -> 9.4 us
  Pallas kernels: 0 us -> 58.7 us
  other arithmetic: 44.2 us -> 0 us
  starting transfers between devices: 24.4 us -> 0 us
  between operations: 16.5 us -> 0.66 us
  matrix products: 14.6 us -> 0 us
    psum x2 -> x0, blocking collectives: 504 us -> none  [the longest x1 495 us: local(): feat_total, filter_total = lax.psum((feat_grad, filter_grad), 'ctx')]
    psum x1 -> x0, waiting for transfers between devices: 297 us -> none  [local(): feat_total, filter_total = lax.psum((feat_grad, filter_grad), 'ctx')]
    gather x4 -> x0, local copies, waits for them, and re-layouts: 249 us -> none  [band_table(): picked = jnp.take(filters, jnp.clip(lagged, 0, FILTER_TAPS - 1), axis=1)]
    pallas_call x0 -> x1, Pallas kernels: none -> 58.7 us  [local(): pl.pallas_call(kernel, out_shape=(grad, grad, grad, jax.ShapeDtypeStruct(...]
    reshape x7 -> x0, local copies, waits for them, and re-layouts: 28.3 us -> none  [the longest x1 14.2 us: skew_sum(): skewed = flattened.reshape(groups, FILTER_TAPS, 2 * FILTER_TAPS + 1)]
    ppermute x7 -> x0, starting transfers between devices: 24.4 us -> none  [passed_along(): lax.ppermute(value, axis, [(source, source + steps) for source in range(l...]
    convert_element_type x8 -> x0, other arithmetic: 14.7 us -> none  [the longest x1 6.29 us: local(): grad_key = adjoint(jnp.concatenate([key_delta, after_key], axis=1), featu...]
    dot_general x6 -> x0, matrix products: 14.6 us -> none  [the longest x1 3.82 us: local(): jnp.einsum('gbnct,gbncs->gts', mid_tiles, current, preferred_element_type...]
  transfers between devices with their start and end apart: 8 -> 0, of which waited for: 1 -> 0; matrix products, arithmetic and copies ran while one was open for 26% -> 0% of each run, Pallas kernels for 0% -> 0%
where the time goes in v1:
time: 69.2 us; the launch traced here: 68.8 us
  Pallas kernels  58.7 us (85%)
  local copies, waits for them, and re-layouts  9.4 us (14%)
    pallas_call x1, Pallas kernels, local(): pl.pallas_call(kernel, out_shape=(grad, grad, grad, jax.ShapeDtypeStruct(...  58.7 us
    unnamed x17, local copies, waits for them, and re-layouts  9.4 us

profile of v1, /device:TPU:1, one launch (start us, length us, event | category | flops | bytes accessed | tf_op | source)
XLA Modules:
  0.0 68.8 jit_solution(608826125520477188)
XLA Ops:
  0.6 0.0 copy-start
  0.6 1.0 %copy-done = bf16[1,256,1024]{2,1,0:T(8,128)(2,1)S(1)} copy-done((bf16[1,256,1024]{2,1,0:T(8,128)(2,1)S(1)}, bf16[1,256,1024]{2,1,0:T(8,128)(2,1)}, u32[]{:S(2)}) %copy-start) | copy-done | bytes 524312
  1.7 0.0 copy-start.1
  1.7 1.0 %copy-done.1 = bf16[1,256,1024]{2,1,0:T(8,128)(2,1)S(1)} copy-done((bf16[1,256,1024]{2,1,0:T(8,128)(2,1)S(1)}, bf16[1,256,1024]{2,1,0:T(8,128)(2,1)}, u32[]{:S(2)}) %copy-start.1) | copy-done | bytes 524312
  2.7 0.0 copy-start.2
  2.7 1.0 %copy-done.2 = bf16[1,256,1024]{2,1,0:T(8,128)(2,1)S(1)} copy-done((bf16[1,256,1024]{2,1,0:T(8,128)(2,1)S(1)}, bf16[1,256,1024]{2,1,0:T(8,128)(2,1)}, u32[]{:S(2)}) %copy-start.2) | copy-done | bytes 524312
  3.8 0.0 copy-start.3
  3.8 1.0 %copy-done.3 = bf16[1,256,1024]{2,1,0:T(8,128)(2,1)S(1)} copy-done((bf16[1,256,1024]{2,1,0:T(8,128)(2,1)S(1)}, bf16[1,256,1024]{2,1,0:T(8,128)(2,1)}, u32[]{:S(2)}) %copy-start.3) | copy-done | bytes 524312
  4.8 0.0 copy-start.4
  4.8 0.9 %copy-done.4 = f32[3,7,1024]{2,1,0:T(8,128)S(1)} copy-done((f32[3,7,1024]{2,1,0:T(8,128)S(1)}, f32[3,7,1024]{2,1,0:T(8,128)}, u32[]{:S(2)}) %copy-start.4) | copy-done | bytes 86040
  5.7 0.0 copy-start.5
  5.7 0.7 %copy-done.5 = bf16[64,128]{1,0:T(8,128)(2,1)S(1)} copy-done((bf16[64,128]{1,0:T(8,128)(2,1)S(1)}, bf16[64,128]{1,0:T(8,128)(2,1)}, u32[]{:S(2)}) %copy-start.5) | copy-done | bytes 16408
  6.4 58.7 %shard_map.101 = (bf16[256,1024]{1,0:T(8,128)(2,1)S(1)}, bf16[256,1024]{1,0:T(8,128)(2,1)S(1)}, bf16[256,1024]{1,0:T(8,128)(2,1)S(1)}, f32[3,7,1024]{2,1,0:T(8,128)S(1)}, f32[64,128]{1,0:T(8,128)S(1)}) custom-call(bf16[256,1024]{1,0:T(8,128)(2,1)S(1)} %bitcast.10, bf16[256,1024]{1,0:T(8,128)(2,1)S(1)} %bitcast.11, bf16[256,1024]{1,0:T(8,128)(2,1)S(1)} %bitcast.12, ...), custom_call_target="tpu_custom_call" | custom-call | flops 805306368 | bytes 3670016 | tf_op jit(solution)/shard_map/pallas_call | solution.py:439
  65.1 0.8 %copy.16 = bf16[1,256,1024]{2,1,0:T(8,128)(2,1)} copy(bf16[1,256,1024]{2,1,0:T(8,128)(2,1)S(1)} %bitcast.9) | data formatting | bytes 1048576
  65.9 0.8 %copy.17 = bf16[1,256,1024]{2,1,0:T(8,128)(2,1)} copy(bf16[1,256,1024]{2,1,0:T(8,128)(2,1)S(1)} %bitcast.8) | data formatting | bytes 1048576
  66.7 0.8 %copy.18 = bf16[1,256,1024]{2,1,0:T(8,128)(2,1)} copy(bf16[1,256,1024]{2,1,0:T(8,128)(2,1)S(1)} %bitcast.7) | data formatting | bytes 1048576
  67.5 0.6 copy.19
  68.2 0.6 copy.20
Async XLA Ops:
  0.6 1.0 %copy-start = (bf16[1,256,1024]{2,1,0:T(8,128)(2,1)S(1)}, bf16[1,256,1024]{2,1,0:T(8,128)(2,1)}, u32[]{:S(2)}) copy-start(bf16[1,256,1024]{2,1,0:T(8,128)(2,1)} %param.6) | copy-start | bytes 1572868
  1.7 1.0 %copy-start.1 = (bf16[1,256,1024]{2,1,0:T(8,128)(2,1)S(1)}, bf16[1,256,1024]{2,1,0:T(8,128)(2,1)}, u32[]{:S(2)}) copy-start(bf16[1,256,1024]{2,1,0:T(8,128)(2,1)} %param.7) | copy-start | bytes 1572868
  2.7 1.0 %copy-start.2 = (bf16[1,256,1024]{2,1,0:T(8,128)(2,1)S(1)}, bf16[1,256,1024]{2,1,0:T(8,128)(2,1)}, u32[]{:S(2)}) copy-start(bf16[1,256,1024]{2,1,0:T(8,128)(2,1)} %param.8) | copy-start | bytes 1572868
  3.8 1.0 %copy-start.3 = (bf16[1,256,1024]{2,1,0:T(8,128)(2,1)S(1)}, bf16[1,256,1024]{2,1,0:T(8,128)(2,1)}, u32[]{:S(2)}) copy-start(bf16[1,256,1024]{2,1,0:T(8,128)(2,1)} %param.9) | copy-start | bytes 1572868
  4.8 0.9 %copy-start.4 = (f32[3,7,1024]{2,1,0:T(8,128)S(1)}, f32[3,7,1024]{2,1,0:T(8,128)}, u32[]{:S(2)}) copy-start(f32[3,7,1024]{2,1,0:T(8,128)} %feat_ref.1) | copy-start | bytes 258052
  5.7 0.7 %copy-start.5 = (bf16[64,128]{1,0:T(8,128)(2,1)S(1)}, bf16[64,128]{1,0:T(8,128)(2,1)}, u32[]{:S(2)}) copy-start(bf16[64,128]{1,0:T(8,128)(2,1)} %filt_ref.1) | copy-start | bytes 49156

commit v2 on v1

v2 whole, which is shorter than its diff:
```python
import jax
import jax.numpy as jnp
from jax import lax
from jax.experimental import pallas as pl
from jax.experimental.pallas import tpu as pltpu
from jax.sharding import PartitionSpec as P

GROUP = 16
TAPS = 7
LAGS = 128
LANES = 128
HALO = 16
BLOCK = 16
WIN = LAGS + BLOCK
CLIP = 100.0
F32 = jnp.float32
BF16 = jnp.bfloat16
MESH = pl.DeviceIdType.MESH
NY, NZ, NX = 4, 16, 4
TEAM = NY * 4
FAR = NZ // 2
CHUNK = 64


def remote(src, dst, send, recv, device):
    return pltpu.make_async_remote_copy(
        src_ref=src, dst_ref=dst, send_sem=send, recv_sem=recv, device_id=device, device_id_type=MESH
    )


def kernel(
    q_hbm,
    k_hbm,
    v_hbm,
    cot_hbm,
    feat_hbm,
    filt_hbm,
    gq_hbm,
    gk_hbm,
    gv_hbm,
    gfeat_ref,
    gfilt_ref,
    gq_ref,
    gk_ref,
    gv_ref,
    q_ref,
    k_ref,
    v_ref,
    cot_ref,
    feat_ref,
    filt_ref,
    tail,
    ahead_raw,
    raw,
    kfeat,
    vfeat,
    prod,
    mid,
    delta,
    tabs,
    fwd_tab,
    rev_tab,
    pair_sums,
    tap_sums,
    pay,
    got,
    ring,
    full,
    norms,
    s_in,
    s_tail,
    r_tail,
    s_ahead,
    r_ahead,
    s_big,
    r_big,
    s_del,
    r_del,
    s_rs,
    r_rs,
    s_far,
    r_far,
    s_ag,
    r_ag,
    s_norm,
    r_norm,
    s_out,
):
    rows = q_ref.shape[0]
    cols = q_ref.shape[1] // LANES
    per_col = LANES // GROUP
    groups = filt_ref.shape[0]
    half = rows // 2
    ctx = lax.axis_index("ctx")
    tp = lax.axis_index("tp")
    n_ctx = 2 * NY * NZ
    core = lax.rem(ctx, 2)
    zi = lax.rem(lax.div(ctx, 2), NZ)
    yi = lax.div(ctx, 2 * NZ)
    z_low = lax.rem(zi, 2)
    z_far = lax.div(zi, 2)

    def at(x, y, z, c):
        return ((y * NZ + z) * 2 + c, x)

    first = ctx == 0
    last = ctx == n_ctx - 1
    after = (lax.rem(ctx + 1, n_ctx), tp)
    before = (lax.rem(ctx + n_ctx - 1, n_ctx), tp)

    def member(dy, dz, dc, x):
        y = lax.rem(yi + dy, NY)
        zl = lax.rem(z_low + dz, 2)
        c = lax.rem(core + dc, 2)
        return (y * 2 + zl) * 2 + c, at(x, y, z_far * 2 + zl, c)

    steps = [(dy, dz, dc) for dy in range(NY) for dz in range(2) for dc in range(2)]
    me = (yi * 2 + z_low) * 2 + core
    team = [member(dy, dz, dc, tp) for dy, dz, dc in steps[1:]]
    senders = [member((NY - dy) % NY, dz, dc, tp)[0] for dy, dz, dc in steps[1:]]
    wide_team = []
    for dx in range(NX):
        for dy, dz, dc in steps:
            if dx or dy or dz or dc:
                device = member(dy, dz, dc, lax.rem(tp + dx, NX))[1]
                index = member((NY - dy) % NY, dz, dc, tp)[0]
                wide_team.append((device, lax.rem(tp + NX - dx, NX) * TEAM + index))
    far = [at(tp, yi, lax.rem(z_far + d, FAR) * 2 + z_low, core) for d in range(1, FAR)]

    barrier = pltpu.get_barrier_semaphore()
    greeted = [after, before] + far + [device for device, _ in wide_team]
    for peer in greeted:
        pl.semaphore_signal(barrier, inc=1, device_id=peer, device_id_type=MESH)

    loads = [
        pltpu.make_async_copy(src, dst, s_in.at[i])
        for i, (src, dst) in enumerate(
            (
                (feat_hbm, feat_ref),
                (k_hbm, k_ref),
                (v_hbm, v_ref),
                (q_hbm, q_ref),
                (cot_hbm, cot_ref),
                (filt_hbm, filt_ref),
            )
        )
    ]
    for copy in loads:
        copy.start()

    def lanes_of(j):
        return pl.ds(pl.multiple_of(j * LANES, LANES), LANES)

    def weights(s, j):
        return [feat_ref[s, pl.ds(tap, 1), lanes_of(j)] for tap in range(TAPS)]

    def featurized(s, j, taps, start, count):
        total = taps[0] * raw[s, j, pl.ds(HALO + start, count), :]
        for tap in range(1, TAPS):
            total = total + taps[tap] * raw[s, j, pl.ds(HALO + start - tap, count), :]
        return total

    def products(j, spans):
        k_taps, v_taps = weights(1, j), weights(2, j)
        for start, count in spans:
            here = pl.ds(start, count)
            k_here = featurized(1, j, k_taps, start, count)
            v_here = featurized(2, j, v_taps, start, count)
            kfeat[j, here, :] = k_here
            vfeat[j, here, :] = v_here
            prod[j, pl.ds(LAGS + start, count), :] = (k_here * v_here).astype(BF16)

    def mids(j, spans):
        q_taps = weights(0, j)
        for start, count in spans:
            here = pl.ds(start, count)
            q_here = featurized(0, j, q_taps, start, count)
            upstream = cot_ref[here, lanes_of(j)].astype(F32)
            mid[j, here, :] = (upstream * q_here).astype(BF16)

    def widen(s, j, ref):
        raw[s, j, pl.ds(HALO, rows), :] = ref[:, lanes_of(j)].astype(F32)

    low_spans = [(HALO, CHUNK - HALO), (CHUNK, CHUNK)]
    high_spans = [(half, CHUNK), (half + CHUNK, CHUNK)]

    for copy in loads[:3]:
        copy.wait()

    @pl.loop(0, cols)
    def _(j):
        widen(1, j, k_ref)
        widen(2, j, v_ref)
        products(j, high_spans)

    for copy in loads[3:]:
        copy.wait()

    pl.semaphore_wait(barrier, len(greeted))

    tails = [
        remote(ref.at[pl.ds(rows - HALO, HALO), :], tail.at[s], s_tail.at[s], r_tail.at[s], after)
        for s, ref in enumerate((q_ref, k_ref, v_ref))
    ]
    aheads = [
        remote(ref.at[pl.ds(0, HALO), :], ahead_raw.at[i], s_ahead.at[i], r_ahead.at[i], before)
        for i, ref in enumerate((q_ref, cot_ref))
    ]
    send_prod = remote(
        prod.at[:, pl.ds(rows, LAGS), :], prod.at[:, pl.ds(0, LAGS), :], s_big.at[0], r_big.at[0], after
    )
    for copy in tails + aheads + [send_prod]:
        copy.start()

    @pl.loop(0, cols)
    def _(j):
        widen(0, j, q_ref)
        mids(j, low_spans)

    send_mid = remote(
        mid.at[:, pl.ds(HALO, LAGS - HALO), :],
        mid.at[:, pl.ds(rows + HALO, LAGS - HALO), :],
        s_big.at[1],
        r_big.at[1],
        before,
    )
    send_mid.start()

    @pl.loop(0, cols)
    def _(j):
        mids(j, high_spans)
        products(j, low_spans)

    lag_row = lax.broadcasted_iota(jnp.int32, (LAGS, 2 * LANES), 0)
    lag_col = lax.broadcasted_iota(jnp.int32, (LAGS, 2 * LANES), 1)
    flip = jnp.where(lag_row + lag_col == LAGS, 1.0, 0.0).astype(BF16)
    keep = jnp.where(lag_row == lag_col, 1.0, 0.0).astype(BF16)
    for pick, table in ((flip, fwd_tab), (keep, rev_tab)):
        wide = jnp.dot(filt_ref[...], pick, preferred_element_type=F32)
        for b in range(BLOCK):
            moved = pltpu.roll(wide, b, 1) if b else wide
            tabs[0, pl.ds(b, groups, stride=BLOCK), :] = moved[:, :LANES]
            tabs[1, pl.ds(b, groups, stride=BLOCK), :] = moved[:, LANES:]
        for j in range(cols):
            span = pl.ds(j * LANES, LANES)
            table[j] = jnp.concatenate([tabs[0, span, :], tabs[1, span, :]], axis=1).astype(BF16)

    for copy in tails + aheads:
        copy.wait_recv()

    @pl.loop(0, cols)
    def _(j):
        for s in range(3):
            behind = tail[s, :, lanes_of(j)].astype(F32)
            raw[s, j, pl.ds(0, HALO), :] = jnp.where(first, 0.0, behind)
        mids(j, [(0, HALO)])
        products(j, [(0, HALO)])
        raw[0, j, pl.ds(HALO + rows, HALO), :] = ahead_raw[0, :, lanes_of(j)].astype(F32)
        q_next = featurized(0, j, weights(0, j), rows, HALO)
        mid_next = ahead_raw[1, :, lanes_of(j)].astype(F32) * q_next
        mid[j, pl.ds(rows, HALO), :] = jnp.where(last, 0.0, mid_next).astype(BF16)

    lane_group = lax.broadcasted_iota(jnp.int32, (BLOCK, LANES), 1) // GROUP
    row_group = lax.broadcasted_iota(jnp.int32, (LANES, 2 * LANES), 0) // BLOCK
    col_group = lax.rem(lax.broadcasted_iota(jnp.int32, (LANES, 2 * LANES), 1), LANES) // GROUP
    own = jnp.where(row_group == col_group, 1.0, 0.0).astype(BF16)
    quarter = half // 2

    def picked(stacked, lane0):
        out = stacked[0:BLOCK, lane0 : lane0 + LANES]
        for g in range(1, per_col):
            piece = stacked[g * BLOCK : (g + 1) * BLOCK, lane0 : lane0 + LANES]
            out = jnp.where(lane_group == g, piece, out)
        return out

    def window(ref, j, start, count):
        near = ref[j, pl.ds(start, count), :]
        far_rows = ref[j, pl.ds(start + quarter, count), :]
        return jnp.concatenate([near, far_rows], axis=1)

    def add_taps(j, s, acc, d, start):
        out = []
        for tap in range(TAPS):
            moved = raw[s, j, pl.ds(HALO + start - tap, BLOCK), :]
            term = jnp.sum((d * moved).reshape(BLOCK // 8, 8, LANES), axis=0)
            out.append(term if acc is None else acc[tap] + term)
        return out

    def forward(j, base):
        band = fwd_tab[j][:, :WIN]
        acc = None
        for a in range(quarter // BLOCK):
            start = base + a * BLOCK
            stacked = jnp.dot(band, window(prod, j, start, WIN), preferred_element_type=F32)
            for side in range(2):
                here = pl.ds(start + side * quarter, BLOCK)
                upstream = cot_ref[here, lanes_of(j)].astype(F32)
                d = upstream * picked(stacked, side * LANES)
                delta[0, j, here, :] = d
                acc = add_taps(j, 0, acc, d, start + side * quarter)
        return acc

    def backward(j, base):
        band = rev_tab[j][:, :WIN]
        acc_k = None
        acc_v = None
        pairs = jnp.zeros((LANES, WIN), F32)
        for a in range(quarter // BLOCK):
            start = base + a * BLOCK
            ahead = window(mid, j, start, WIN)
            stacked = jnp.dot(band, ahead, preferred_element_type=F32)
            for side in range(2):
                here = pl.ds(start + side * quarter, BLOCK)
                pg = picked(stacked, side * LANES)
                dk = pg * vfeat[j, here, :]
                dv = pg * kfeat[j, here, :]
                delta[1, j, here, :] = dk
                delta[2, j, here, :] = dv
                acc_k = add_taps(j, 1, acc_k, dk, start + side * quarter)
                acc_v = add_taps(j, 2, acc_v, dv, start + side * quarter)
            base_rows = window(prod, j, LAGS + start, BLOCK)
            spread = jnp.concatenate([base_rows] * per_col, axis=0) * own
            pairs = pairs + lax.dot_general(
                spread, ahead, (((1,), (1,)), ((), ())), preferred_element_type=F32
            )
        return acc_k + acc_v, pairs

    @pl.loop(0, cols)
    def _(j):
        acc = forward(j, half)
        more, pairs = backward(j, 0)
        for i, value in enumerate(acc + more):
            tap_sums[j, i] = value
        pair_sums[j, :, :WIN] = pairs

    send_prod.wait_recv()
    send_mid.wait_recv()

    @pl.when(first)
    def _():
        prod[:, pl.ds(0, LAGS), :] = jnp.zeros((cols, LAGS, LANES), BF16)

    @pl.when(last)
    def _():
        mid[:, pl.ds(rows + HALO, LAGS - HALO), :] = jnp.zeros((cols, LAGS - HALO, LANES), BF16)

    @pl.loop(0, cols)
    def _(j):
        acc = forward(j, 0)
        more, pairs = backward(j, half)
        for i, value in enumerate(acc + more):
            row = jnp.sum(tap_sums[j, i] + value, axis=0, keepdims=True)
            s, tap = i // TAPS, i % TAPS
            pay[2 * j + s // 2, pl.ds((s % 2) * 8 + tap, 1), :] = row
        for s in range(3):
            pay[2 * j + s // 2, pl.ds((s % 2) * 8 + TAPS, 1), :] = jnp.zeros((1, LANES), F32)
        pairs = pairs + pair_sums[j, :, :WIN]
        tabs[0, pl.ds(0, LANES), :] = pairs[:, :LANES]
        tabs[1, pl.ds(0, LANES), :BLOCK] = pairs[:, LANES:]
        lags = tabs[0, pl.ds(0, per_col, stride=BLOCK), :]
        for b in range(1, BLOCK):
            low = tabs[0, pl.ds(b, per_col, stride=BLOCK), :]
            high = tabs[1, pl.ds(b, per_col, stride=BLOCK), :]
            both = pltpu.roll(jnp.concatenate([low, high], axis=1), 2 * LANES - b, 1)
            lags = lags + both[:, :LANES]
        pay[2 * j + 1, pl.ds(8, per_col), :] = lags

    scatter = [
        remote(pay.at[index], got.at[i], s_rs.at[i], r_rs.at[i], device)
        for i, (index, device) in enumerate(team)
    ]
    for copy in scatter:
        copy.start()

    send_del = remote(
        delta.at[:, :, pl.ds(0, 8), :], delta.at[:, :, pl.ds(rows, 8), :], s_del.at[0], r_del.at[0], before
    )
    send_del.start()

    def adjoint(s, out_ref, spans):
        @pl.loop(0, cols)
        def _(j):
            taps = weights(s, j)
            for start, count in spans:
                total = taps[0] * delta[s, j, pl.ds(start, count), :]
                for tap in range(1, TAPS):
                    total = total + taps[tap] * delta[s, j, pl.ds(start + tap, count), :]
                out_ref[pl.ds(start, count), lanes_of(j)] = total.astype(BF16)

    body_spans = [(0, CHUNK), (CHUNK, CHUNK), (2 * CHUNK, CHUNK), (3 * CHUNK, CHUNK - HALO)]
    adjoint(0, gq_ref, body_spans)
    adjoint(1, gk_ref, body_spans)
    adjoint(2, gv_ref, body_spans)

    for copy in scatter:
        copy.wait_recv()
    mine = pay[me]
    for i in range(len(team)):
        mine = mine + got[i]
    ring[z_far] = mine
    spread_far = [
        remote(ring.at[z_far], ring.at[z_far], s_far.at[i], r_far.at[i], device)
        for i, device in enumerate(far)
    ]
    for copy in spread_far:
        copy.start()

    send_del.wait_recv()

    @pl.when(last)
    def _():
        delta[:, :, pl.ds(rows, 8), :] = jnp.zeros((3, cols, 8, LANES), F32)

    for s, out_ref in enumerate((gq_ref, gk_ref, gv_ref)):
        adjoint(s, out_ref, [(rows - HALO, HALO)])
    stores = [
        pltpu.make_async_copy(src, dst, s_out.at[i])
        for i, (src, dst) in enumerate(((gq_ref, gq_hbm), (gk_ref, gk_hbm), (gv_ref, gv_hbm)))
    ]
    for copy in stores:
        copy.start()

    for i, device in enumerate(far):
        src = lax.rem(z_far + FAR - 1 - i, FAR)
        remote(ring.at[src], ring.at[src], s_far.at[i], r_far.at[i], device).wait_recv()
    mine = ring[0]
    for i in range(1, FAR):
        mine = mine + ring[i]
    full[me] = mine
    gather = [
        remote(full.at[me], full.at[me], s_ag.at[i], r_ag.at[i], device) for i, (_, device) in enumerate(team)
    ]
    for copy in gather:
        copy.start()
    squares = jnp.sum(jnp.sum(mine * mine, axis=0, keepdims=True), axis=1, keepdims=True)
    seat = tp * TEAM + me
    norms[seat] = jnp.broadcast_to(squares, (1, LANES))
    tell = [
        remote(norms.at[seat], norms.at[seat], s_norm.at[i], r_norm.at[i], device)
        for i, (device, _) in enumerate(wide_team)
    ]
    for copy in tell:
        copy.start()
    for i, (_, device) in enumerate(team):
        remote(full.at[senders[i]], full.at[senders[i]], s_ag.at[i], r_ag.at[i], device).wait_recv()
    for i, (device, src) in enumerate(wide_team):
        remote(norms.at[src], norms.at[src], s_norm.at[i], r_norm.at[i], device).wait_recv()
    total = norms[0]
    for i in range(1, NX * TEAM):
        total = total + norms[i]
    scale = 1.0 / jnp.maximum(1.0, jnp.sqrt(total) / CLIP)
    for j in range(cols):
        for s in range(3):
            gfeat_ref[s, :, pl.ds(j * LANES, LANES)] = scale * full[2 * j + s // 2, pl.ds((s % 2) * 8, TAPS), :]
        gfilt_ref[pl.ds(j * per_col, per_col), :] = scale * full[2 * j + 1, pl.ds(8, per_col), :]

    for copy in tails + aheads + [send_prod, send_mid, send_del] + scatter + spread_far + gather + tell:
        copy.wait_send()
    for copy in stores:
        copy.wait()


def emit(*refs):
    count = 5
    sources, targets, held = refs[:count], refs[count : 2 * count], refs[2 * count : 3 * count]
    s_in, s_out = refs[3 * count :]
    loads = [pltpu.make_async_copy(sources[i], held[i], s_in.at[i]) for i in range(count)]
    stores = [pltpu.make_async_copy(held[i], targets[i], s_out.at[i]) for i in range(count)]
    for copy in loads:
        copy.start()
    for load, store in zip(loads, stores):
        load.wait()
        store.start()
    for copy in stores:
        copy.wait()


def local(query_raw, key_raw, value_raw, cotangent, featurizer, filters):
    _, rows, channels = query_raw.shape
    groups = filters.shape[0]
    cols = channels // LANES
    flat = lambda x: x.reshape(rows, channels)
    vmem = pl.BlockSpec(memory_space=pltpu.VMEM)
    hbm = pl.BlockSpec(memory_space=pltpu.HBM)
    grad = jax.ShapeDtypeStruct((rows, channels), BF16)
    dma = pltpu.SemaphoreType.DMA
    shapes = (
        grad,
        grad,
        grad,
        jax.ShapeDtypeStruct(featurizer.shape, F32),
        jax.ShapeDtypeStruct(filters.shape, F32),
    )
    outs = pl.pallas_call(
        kernel,
        out_shape=shapes,
        in_specs=[hbm] * 6,
        out_specs=(hbm,) * 3 + (vmem,) * 2,
        scratch_shapes=[
            pltpu.VMEM((rows, channels), BF16),
            pltpu.VMEM((rows, channels), BF16),
            pltpu.VMEM((rows, channels), BF16),
            pltpu.VMEM((rows, channels), BF16),
            pltpu.VMEM((rows, channels), BF16),
            pltpu.VMEM((rows, channels), BF16),
            pltpu.VMEM((rows, channels), BF16),
            pltpu.VMEM(featurizer.shape, F32),
            pltpu.VMEM(filters.shape, BF16),
            pltpu.VMEM((3, HALO, channels), BF16),
            pltpu.VMEM((2, HALO, channels), BF16),
            pltpu.VMEM((3, cols, HALO + rows + HALO, LANES), F32),
            pltpu.VMEM((cols, rows, LANES), F32),
            pltpu.VMEM((cols, rows, LANES), F32),
            pltpu.VMEM((cols, LAGS + rows, LANES), BF16),
            pltpu.VMEM((cols, LAGS + rows, LANES), BF16),
            pltpu.VMEM((3, cols, rows + 8, LANES), F32),
            pltpu.VMEM((2, groups * BLOCK, LANES), F32),
            pltpu.VMEM((cols, LANES, 2 * LANES), BF16),
            pltpu.VMEM((cols, LANES, 2 * LANES), BF16),
            pltpu.VMEM((cols, LANES, 2 * LANES), F32),
            pltpu.VMEM((cols, 3 * TAPS, 8, LANES), F32),
            pltpu.VMEM((TEAM, 16, LANES), F32),
            pltpu.VMEM((TEAM - 1, 16, LANES), F32),
            pltpu.VMEM((FAR, 16, LANES), F32),
            pltpu.VMEM((TEAM, 16, LANES), F32),
            pltpu.VMEM((NX * TEAM, 1, LANES), F32),
            dma((6,)),
            dma((3,)),
            dma((3,)),
            dma((2,)),
            dma((2,)),
            dma((2,)),
            dma((2,)),
            dma((1,)),
            dma((1,)),
            dma((TEAM - 1,)),
            dma((TEAM - 1,)),
            dma((FAR - 1,)),
            dma((FAR - 1,)),
            dma((TEAM - 1,)),
            dma((TEAM - 1,)),
            dma((NX * TEAM - 1,)),
            dma((NX * TEAM - 1,)),
            dma((3,)),
        ],
        compiler_params=pltpu.CompilerParams(
            collective_id=0, has_side_effects=True, vmem_limit_bytes=60 * 1024 * 1024
        ),
        cost_estimate=pl.CostEstimate(
            flops=12 * 256 * rows * channels, bytes_accessed=14 * rows * channels, transcendentals=0
        ),
    )(flat(query_raw), flat(key_raw), flat(value_raw), flat(cotangent), featurizer, filters)
    outs = pl.pallas_call(
        emit,
        out_shape=shapes,
        in_specs=[hbm] * 5,
        out_specs=(hbm,) * 5,
        scratch_shapes=[pltpu.VMEM(shape.shape, shape.dtype) for shape in shapes] + [dma((5,)), dma((5,))],
        compiler_params=pltpu.CompilerParams(vmem_limit_bytes=60 * 1024 * 1024),
    )(*outs)
    shape = query_raw.shape
    return (outs[0].reshape(shape), outs[1].reshape(shape), outs[2].reshape(shape), outs[3], outs[4])


def solution(mesh):
    stream = P(None, "ctx", "tp")
    return jax.shard_map(
        local,
        mesh=mesh,
        in_specs=(stream, stream, stream, stream, P(None, None, "tp"), P("tp", None)),
        out_specs=(stream, stream, stream, P(None, None, "tp"), P("tp", None)),
        check_vma=False,
    )
```

time: 69.2 us -> 51.3 us (0.74)
  local copies, waits for them, and re-layouts: 9.4 us -> 0 us
  Pallas kernels: 58.7 us -> 50.5 us
    unnamed x17 -> x0, local copies, waits for them, and re-layouts: 9.4 us -> none
    pallas_call x1 -> x2, Pallas kernels: 58.7 us -> 50.5 us  [the longest x1 48.2 us: local(): pl.pallas_call(kernel, out_shape=shapes, in_specs=[hbm] * 6, out_specs=(h...]
where the time goes in v2:
time: 51.3 us; the launch traced here: 51.1 us
  Pallas kernels  50.5 us (98%)
  between operations  0.64 us (1%)
    pallas_call x1, Pallas kernels, local(): pl.pallas_call(kernel, out_shape=shapes, in_specs=[hbm] * 6, out_specs=(h...  48.2 us
    pallas_call x1, Pallas kernels, local(): pl.pallas_call(emit, out_shape=shapes, in_specs=[hbm] * 5, out_specs=(hbm...  2.29 us

profile of v2, /device:TPU:1, one launch (start us, length us, event | category | flops | bytes accessed | tf_op | source)
XLA Modules:
  0.0 51.1 jit_solution(2128721149659505747)
XLA Ops:
  0.6 48.2 %shard_map.101 = (bf16[256,1024]{1,0:T(8,128)(2,1)}, bf16[256,1024]{1,0:T(8,128)(2,1)}, bf16[256,1024]{1,0:T(8,128)(2,1)}, f32[3,7,1024]{2,1,0:T(8,128)}, f32[64,128]{1,0:T(8,128)}) custom-call(bf16[256,1024]{1,0:T(8,128)(2,1)} %bitcast.7, bf16[256,1024]{1,0:T(8,128)(2,1)} %bitcast.8, bf16[256,1024]{1,0:T(8,128)(2,1)} %bitcast.9, ...), custom_call_target="tpu_custom_call" | custom-call | flops 805306368 | bytes 3670016 | tf_op jit(solution)/shard_map/pallas_call | solution.py:494
  48.8 2.3 %shard_map.102 = (bf16[256,1024]{1,0:T(8,128)(2,1)}, bf16[256,1024]{1,0:T(8,128)(2,1)}, bf16[256,1024]{1,0:T(8,128)(2,1)}, f32[3,7,1024]{2,1,0:T(8,128)}, f32[64,128]{1,0:T(8,128)}) custom-call(bf16[256,1024]{1,0:T(8,128)(2,1)} %get-tuple-element.15.refs_0_, bf16[256,1024]{1,0:T(8,128)(2,1)} %get-tuple-element.16.refs_1_, ...), custom_call_target="tpu_custom_call" | custom-call | tf_op jit(solution)/shard_map/pallas_call | solution.py:553

commit v3 on v2

--- a/solution.py
+++ b/solution.py
@@ -72,8 +72,10 @@
     r_tail,
     s_ahead,
     r_ahead,
-    s_big,
-    r_big,
+    s_prod,
+    r_prod,
+    s_mid,
+    r_mid,
     s_del,
     r_del,
     s_rs,
@@ -85,6 +87,7 @@
     s_norm,
     r_norm,
     s_out,
+    hear,
 ):
     rows = q_ref.shape[0]
     cols = q_ref.shape[1] // LANES
@@ -128,7 +131,10 @@
     far = [at(tp, yi, lax.rem(z_far + d, FAR) * 2 + z_low, core) for d in range(1, FAR)]
 
     barrier = pltpu.get_barrier_semaphore()
-    greeted = [after, before] + far + [device for device, _ in wide_team]
+    x_peers = [at(lax.rem(tp + d, NX), yi, zi, core) for d in range(1, NX)]
+    z_two = [at(tp, yi, lax.rem(zi + d, NZ), core) for d in (2, NZ - 2)]
+    z_four = [at(tp, yi, lax.rem(zi + d, NZ), core) for d in (4, NZ - 4)]
+    greeted = [after, before] + [device for _, device in team] + x_peers + z_two
     for peer in greeted:
         pl.semaphore_signal(barrier, inc=1, device_id=peer, device_id_type=MESH)
 
@@ -198,6 +204,9 @@
 
     pl.semaphore_wait(barrier, len(greeted))
 
+    for peer in x_peers + z_two:
+        pl.semaphore_signal(hear.at[0], inc=1, device_id=peer, device_id_type=MESH)
+
     tails = [
         remote(ref.at[pl.ds(rows - HALO, HALO), :], tail.at[s], s_tail.at[s], r_tail.at[s], after)
         for s, ref in enumerate((q_ref, k_ref, v_ref))
@@ -206,25 +215,32 @@
         remote(ref.at[pl.ds(0, HALO), :], ahead_raw.at[i], s_ahead.at[i], r_ahead.at[i], before)
         for i, ref in enumerate((q_ref, cot_ref))
     ]
-    send_prod = remote(
-        prod.at[:, pl.ds(rows, LAGS), :], prod.at[:, pl.ds(0, LAGS), :], s_big.at[0], r_big.at[0], after
-    )
-    for copy in tails + aheads + [send_prod]:
-        copy.start()
+    for copy in tails + aheads:
+        copy.start()
+
+    def prod_copy(j):
+        return remote(
+            prod.at[j, pl.ds(rows, LAGS), :], prod.at[j, pl.ds(0, LAGS), :], s_prod.at[j], r_prod.at[j], after
+        )
+
+    def mid_copy(j):
+        return remote(
+            mid.at[j, pl.ds(HALO, LAGS - HALO), :],
+            mid.at[j, pl.ds(rows + HALO, LAGS - HALO), :],
+            s_mid.at[j],
+            r_mid.at[j],
+            before,
+        )
+
+    @pl.loop(0, cols)
+    def _(j):
+        prod_copy(j).start()
 
     @pl.loop(0, cols)
     def _(j):
         widen(0, j, q_ref)
         mids(j, low_spans)
-
-    send_mid = remote(
-        mid.at[:, pl.ds(HALO, LAGS - HALO), :],
-        mid.at[:, pl.ds(rows + HALO, LAGS - HALO), :],
-        s_big.at[1],
-        r_big.at[1],
-        before,
-    )
-    send_mid.start()
+        mid_copy(j).start()
 
     @pl.loop(0, cols)
     def _(j):
@@ -333,19 +349,23 @@
             tap_sums[j, i] = value
         pair_sums[j, :, :WIN] = pairs
 
-    send_prod.wait_recv()
-    send_mid.wait_recv()
-
-    @pl.when(first)
-    def _():
-        prod[:, pl.ds(0, LAGS), :] = jnp.zeros((cols, LAGS, LANES), BF16)
-
-    @pl.when(last)
-    def _():
-        mid[:, pl.ds(rows + HALO, LAGS - HALO), :] = jnp.zeros((cols, LAGS - HALO, LANES), BF16)
-
-    @pl.loop(0, cols)
-    def _(j):
+    pl.semaphore_wait(hear.at[0], len(x_peers + z_two))
+    for peer in z_four:
+        pl.semaphore_signal(hear.at[1], inc=1, device_id=peer, device_id_type=MESH)
+
+    @pl.loop(0, cols)
+    def _(j):
+        prod_copy(j).wait_recv()
+        mid_copy(j).wait_recv()
+
+        @pl.when(first)
+        def _():
+            prod[j, pl.ds(0, LAGS), :] = jnp.zeros((LAGS, LANES), BF16)
+
+        @pl.when(last)
+        def _():
+            mid[j, pl.ds(rows + HALO, LAGS - HALO), :] = jnp.zeros((LAGS - HALO, LANES), BF16)
+
         acc = forward(j, 0)
         more, pairs = backward(j, half)
         for i, value in enumerate(acc + more):
@@ -402,6 +422,7 @@
         remote(ring.at[z_far], ring.at[z_far], s_far.at[i], r_far.at[i], device)
         for i, device in enumerate(far)
     ]
+    pl.semaphore_wait(hear.at[1], len(z_four))
     for copy in spread_far:
         copy.start()
 
@@ -454,7 +475,12 @@
             gfeat_ref[s, :, pl.ds(j * LANES, LANES)] = scale * full[2 * j + s // 2, pl.ds((s % 2) * 8, TAPS), :]
         gfilt_ref[pl.ds(j * per_col, per_col), :] = scale * full[2 * j + 1, pl.ds(8, per_col), :]
 
-    for copy in tails + aheads + [send_prod, send_mid, send_del] + scatter + spread_far + gather + tell:
+    @pl.loop(0, cols)
+    def _(j):
+        prod_copy(j).wait_send()
+        mid_copy(j).wait_send()
+
+    for copy in tails + aheads + [send_del] + scatter + spread_far + gather + tell:
         copy.wait_send()
     for copy in stores:
         copy.wait()
@@ -529,8 +555,10 @@
             dma((3,)),
             dma((2,)),
             dma((2,)),
-            dma((2,)),
-            dma((2,)),
+            dma((cols,)),
+            dma((cols,)),
+            dma((cols,)),
+            dma((cols,)),
             dma((1,)),
             dma((1,)),
             dma((TEAM - 1,)),
@@ -542,6 +570,7 @@
             dma((NX * TEAM - 1,)),
             dma((NX * TEAM - 1,)),
             dma((3,)),
+            pltpu.SemaphoreType.REGULAR((2,)),
         ],
         compiler_params=pltpu.CompilerParams(
             collective_id=0, has_side_effects=True, vmem_limit_bytes=60 * 1024 * 1024

time: 51.3 us -> 49.6 us (0.967)
  Pallas kernels: 50.5 us -> 48.7 us
    pallas_call x1, Pallas kernels: 48.2 us -> 46.4 us  [local(): pl.pallas_call(kernel, out_shape=shapes, in_specs=[hbm] * 6, out_specs=(h...]
where the time goes in v3:
time: 49.6 us; the launch traced here: 49.4 us
  Pallas kernels  48.7 us (98%)
  between operations  0.64 us (1%)
    pallas_call x1, Pallas kernels, local(): pl.pallas_call(kernel, out_shape=shapes, in_specs=[hbm] * 6, out_specs=(h...  46.4 us
    pallas_call x1, Pallas kernels, local(): pl.pallas_call(emit, out_shape=shapes, in_specs=[hbm] * 5, out_specs=(hbm...  2.29 us

profile of v3, /device:TPU:1, one launch (start us, length us, event | category | flops | bytes accessed | tf_op | source)
XLA Modules:
  0.0 49.4 jit_solution(16197768681751753811)
XLA Ops:
  0.6 46.4 %shard_map.101 = (bf16[256,1024]{1,0:T(8,128)(2,1)}, bf16[256,1024]{1,0:T(8,128)(2,1)}, bf16[256,1024]{1,0:T(8,128)(2,1)}, f32[3,7,1024]{2,1,0:T(8,128)}, f32[64,128]{1,0:T(8,128)}) custom-call(bf16[256,1024]{1,0:T(8,128)(2,1)} %bitcast.7, bf16[256,1024]{1,0:T(8,128)(2,1)} %bitcast.8, bf16[256,1024]{1,0:T(8,128)(2,1)} %bitcast.9, ...), custom_call_target="tpu_custom_call" | custom-call | flops 805306368 | bytes 3670016 | tf_op jit(solution)/shard_map/pallas_call | solution.py:520
  47.1 2.3 %shard_map.102 = (bf16[256,1024]{1,0:T(8,128)(2,1)}, bf16[256,1024]{1,0:T(8,128)(2,1)}, bf16[256,1024]{1,0:T(8,128)(2,1)}, f32[3,7,1024]{2,1,0:T(8,128)}, f32[64,128]{1,0:T(8,128)}) custom-call(bf16[256,1024]{1,0:T(8,128)(2,1)} %get-tuple-element.15.refs_0_, bf16[256,1024]{1,0:T(8,128)(2,1)} %get-tuple-element.16.refs_1_, ...), custom_call_target="tpu_custom_call" | custom-call | tf_op jit(solution)/shard_map/pallas_call | solution.py:582

commit v4 on v3

--- a/solution.py
+++ b/solution.py
@@ -12,6 +12,7 @@
 HALO = 16
 BLOCK = 16
 WIN = LAGS + BLOCK
+STACK = LANES // GROUP * BLOCK
 CLIP = 100.0
 F32 = jnp.float32
 BF16 = jnp.bfloat16
@@ -26,6 +27,13 @@
     return pltpu.make_async_remote_copy(
         src_ref=src, dst_ref=dst, send_sem=send, recv_sem=recv, device_id=device, device_id_type=MESH
     )
+
+
+def added(terms):
+    terms = [term.astype(F32) for term in terms]
+    while len(terms) > 1:
+        terms = [a + b for a, b in zip(terms[::2], terms[1::2])] + terms[len(terms) & ~1 :]
+    return terms[0]
 
 
 def kernel(
@@ -60,7 +68,6 @@
     tabs,
     fwd_tab,
     rev_tab,
-    pair_sums,
     tap_sums,
     pay,
     got,
@@ -142,12 +149,12 @@
         pltpu.make_async_copy(src, dst, s_in.at[i])
         for i, (src, dst) in enumerate(
             (
-                (feat_hbm, feat_ref),
+                (filt_hbm, filt_ref),
                 (k_hbm, k_ref),
                 (v_hbm, v_ref),
+                (feat_hbm, feat_ref),
                 (q_hbm, q_ref),
                 (cot_hbm, cot_ref),
-                (filt_hbm, filt_ref),
             )
         )
     ]
@@ -190,62 +197,7 @@
     low_spans = [(HALO, CHUNK - HALO), (CHUNK, CHUNK)]
     high_spans = [(half, CHUNK), (half + CHUNK, CHUNK)]
 
-    for copy in loads[:3]:
-        copy.wait()
-
-    @pl.loop(0, cols)
-    def _(j):
-        widen(1, j, k_ref)
-        widen(2, j, v_ref)
-        products(j, high_spans)
-
-    for copy in loads[3:]:
-        copy.wait()
-
-    pl.semaphore_wait(barrier, len(greeted))
-
-    for peer in x_peers + z_two:
-        pl.semaphore_signal(hear.at[0], inc=1, device_id=peer, device_id_type=MESH)
-
-    tails = [
-        remote(ref.at[pl.ds(rows - HALO, HALO), :], tail.at[s], s_tail.at[s], r_tail.at[s], after)
-        for s, ref in enumerate((q_ref, k_ref, v_ref))
-    ]
-    aheads = [
-        remote(ref.at[pl.ds(0, HALO), :], ahead_raw.at[i], s_ahead.at[i], r_ahead.at[i], before)
-        for i, ref in enumerate((q_ref, cot_ref))
-    ]
-    for copy in tails + aheads:
-        copy.start()
-
-    def prod_copy(j):
-        return remote(
-            prod.at[j, pl.ds(rows, LAGS), :], prod.at[j, pl.ds(0, LAGS), :], s_prod.at[j], r_prod.at[j], after
-        )
-
-    def mid_copy(j):
-        return remote(
-            mid.at[j, pl.ds(HALO, LAGS - HALO), :],
-            mid.at[j, pl.ds(rows + HALO, LAGS - HALO), :],
-            s_mid.at[j],
-            r_mid.at[j],
-            before,
-        )
-
-    @pl.loop(0, cols)
-    def _(j):
-        prod_copy(j).start()
-
-    @pl.loop(0, cols)
-    def _(j):
-        widen(0, j, q_ref)
-        mids(j, low_spans)
-        mid_copy(j).start()
-
-    @pl.loop(0, cols)
-    def _(j):
-        mids(j, high_spans)
-        products(j, low_spans)
+    loads[0].wait()
 
     lag_row = lax.broadcasted_iota(jnp.int32, (LAGS, 2 * LANES), 0)
     lag_col = lax.broadcasted_iota(jnp.int32, (LAGS, 2 * LANES), 1)
@@ -258,8 +210,65 @@
             tabs[0, pl.ds(b, groups, stride=BLOCK), :] = moved[:, :LANES]
             tabs[1, pl.ds(b, groups, stride=BLOCK), :] = moved[:, LANES:]
         for j in range(cols):
-            span = pl.ds(j * LANES, LANES)
+            span = pl.ds(j * STACK, STACK)
             table[j] = jnp.concatenate([tabs[0, span, :], tabs[1, span, :]], axis=1).astype(BF16)
+
+    for copy in loads[1:4]:
+        copy.wait()
+
+    @pl.loop(0, cols)
+    def _(j):
+        widen(1, j, k_ref)
+        widen(2, j, v_ref)
+        products(j, high_spans)
+
+    for copy in loads[4:]:
+        copy.wait()
+
+    pl.semaphore_wait(barrier, len(greeted))
+
+    for peer in x_peers + z_two:
+        pl.semaphore_signal(hear.at[0], inc=1, device_id=peer, device_id_type=MESH)
+
+    tails = [
+        remote(ref.at[pl.ds(rows - HALO, HALO), :], tail.at[s], s_tail.at[s], r_tail.at[s], after)
+        for s, ref in enumerate((q_ref, k_ref, v_ref))
+    ]
+    aheads = [
+        remote(ref.at[pl.ds(0, HALO), :], ahead_raw.at[i], s_ahead.at[i], r_ahead.at[i], before)
+        for i, ref in enumerate((q_ref, cot_ref))
+    ]
+    for copy in tails + aheads:
+        copy.start()
+
+    def prod_copy(j):
+        return remote(
+            prod.at[j, pl.ds(rows, LAGS), :], prod.at[j, pl.ds(0, LAGS), :], s_prod.at[j], r_prod.at[j], after
+        )
+
+    def mid_copy(j):
+        return remote(
+            mid.at[j, pl.ds(HALO, LAGS - HALO), :],
+            mid.at[j, pl.ds(rows + HALO, LAGS - HALO), :],
+            s_mid.at[j],
+            r_mid.at[j],
+            before,
+        )
+
+    @pl.loop(0, cols)
+    def _(j):
+        prod_copy(j).start()
+
+    @pl.loop(0, cols)
+    def _(j):
+        widen(0, j, q_ref)
+        mids(j, low_spans)
+        mid_copy(j).start()
+
+    @pl.loop(0, cols)
+    def _(j):
+        mids(j, high_spans)
+        products(j, low_spans)
 
     for copy in tails + aheads:
         copy.wait_recv()
@@ -277,8 +286,8 @@
         mid[j, pl.ds(rows, HALO), :] = jnp.where(last, 0.0, mid_next).astype(BF16)
 
     lane_group = lax.broadcasted_iota(jnp.int32, (BLOCK, LANES), 1) // GROUP
-    row_group = lax.broadcasted_iota(jnp.int32, (LANES, 2 * LANES), 0) // BLOCK
-    col_group = lax.rem(lax.broadcasted_iota(jnp.int32, (LANES, 2 * LANES), 1), LANES) // GROUP
+    row_group = lax.broadcasted_iota(jnp.int32, (STACK, 2 * LANES), 0) // BLOCK
+    col_group = lax.rem(lax.broadcasted_iota(jnp.int32, (STACK, 2 * LANES), 1), LANES) // GROUP
     own = jnp.where(row_group == col_group, 1.0, 0.0).astype(BF16)
     quarter = half // 2
 
@@ -320,7 +329,7 @@
         band = rev_tab[j][:, :WIN]
         acc_k = None
         acc_v = None
-        pairs = jnp.zeros((LANES, WIN), F32)
+        pairs = jnp.zeros((STACK, WIN), F32)
         for a in range(quarter // BLOCK):
             start = base + a * BLOCK
             ahead = window(mid, j, start, WIN)
@@ -341,19 +350,28 @@
             )
         return acc_k + acc_v, pairs
 
-    @pl.loop(0, cols)
+    def tap_rows(j, i):
+        return pl.ds(pl.multiple_of((j * 24 + i // TAPS * 8 + i % TAPS) * 8, 8), 8)
+
+    def tile_rows(j):
+        return pl.ds(pl.multiple_of(j * STACK, STACK), STACK)
+
+    @pl.loop(0, cols, unroll=4)
     def _(j):
         acc = forward(j, half)
         more, pairs = backward(j, 0)
         for i, value in enumerate(acc + more):
-            tap_sums[j, i] = value
-        pair_sums[j, :, :WIN] = pairs
+            tap_sums[tap_rows(j, i), :] = value
+        for s in range(3):
+            tap_sums[pl.ds(pl.multiple_of((j * 24 + s * 8 + TAPS) * 8, 8), 8), :] = jnp.zeros((8, LANES), F32)
+        tabs[0, tile_rows(j), :] = pairs[:, :LANES]
+        tabs[1, tile_rows(j), :BLOCK] = pairs[:, LANES:]
 
     pl.semaphore_wait(hear.at[0], len(x_peers + z_two))
     for peer in z_four:
         pl.semaphore_signal(hear.at[1], inc=1, device_id=peer, device_id_type=MESH)
 
-    @pl.loop(0, cols)
+    @pl.loop(0, cols, unroll=4)
     def _(j):
         prod_copy(j).wait_recv()
         mid_copy(j).wait_recv()
@@ -369,21 +387,24 @@
         acc = forward(j, 0)
         more, pairs = backward(j, half)
         for i, value in enumerate(acc + more):
-            row = jnp.sum(tap_sums[j, i] + value, axis=0, keepdims=True)
-            s, tap = i // TAPS, i % TAPS
-            pay[2 * j + s // 2, pl.ds((s % 2) * 8 + tap, 1), :] = row
-        for s in range(3):
-            pay[2 * j + s // 2, pl.ds((s % 2) * 8 + TAPS, 1), :] = jnp.zeros((1, LANES), F32)
-        pairs = pairs + pair_sums[j, :, :WIN]
-        tabs[0, pl.ds(0, LANES), :] = pairs[:, :LANES]
-        tabs[1, pl.ds(0, LANES), :BLOCK] = pairs[:, LANES:]
-        lags = tabs[0, pl.ds(0, per_col, stride=BLOCK), :]
-        for b in range(1, BLOCK):
-            low = tabs[0, pl.ds(b, per_col, stride=BLOCK), :]
-            high = tabs[1, pl.ds(b, per_col, stride=BLOCK), :]
-            both = pltpu.roll(jnp.concatenate([low, high], axis=1), 2 * LANES - b, 1)
-            lags = lags + both[:, :LANES]
-        pay[2 * j + 1, pl.ds(8, per_col), :] = lags
+            tap_sums[tap_rows(j, i), :] += value
+        tabs[0, tile_rows(j), :] += pairs[:, :LANES]
+        tabs[1, tile_rows(j), :BLOCK] += pairs[:, LANES:]
+
+    taps_total = tap_sums[pl.ds(0, cols * 24, stride=8), :]
+    for b in range(1, 8):
+        taps_total = taps_total + tap_sums[pl.ds(b, cols * 24, stride=8), :]
+    lane = lax.broadcasted_iota(jnp.int32, (groups, LANES), 1)
+    lags = tabs[0, pl.ds(0, groups, stride=BLOCK), :]
+    for b in range(1, BLOCK):
+        low = tabs[0, pl.ds(b, groups, stride=BLOCK), :]
+        high = tabs[1, pl.ds(b, groups, stride=BLOCK), :]
+        lags = lags + pltpu.roll(jnp.where(lane >= b, low, high), LANES - b, 1)
+    for j in range(cols):
+        pay[2 * j] = taps_total[j * 24 : j * 24 + 16].astype(BF16)
+        pay[2 * j + 1] = jnp.concatenate(
+            [taps_total[j * 24 + 16 : j * 24 + 24], lags[j * per_col : (j + 1) * per_col]], axis=0
+        ).astype(BF16)
 
     scatter = [
         remote(pay.at[index], got.at[i], s_rs.at[i], r_rs.at[i], device)
@@ -414,10 +435,8 @@
 
     for copy in scatter:
         copy.wait_recv()
-    mine = pay[me]
-    for i in range(len(team)):
-        mine = mine + got[i]
-    ring[z_far] = mine
+    mine = added([pay[me]] + [got[i] for i in range(len(team))])
+    ring[z_far] = mine.astype(BF16)
     spread_far = [
         remote(ring.at[z_far], ring.at[z_far], s_far.at[i], r_far.at[i], device)
         for i, device in enumerate(far)
@@ -444,10 +463,8 @@
     for i, device in enumerate(far):
         src = lax.rem(z_far + FAR - 1 - i, FAR)
         remote(ring.at[src], ring.at[src], s_far.at[i], r_far.at[i], device).wait_recv()
-    mine = ring[0]
-    for i in range(1, FAR):
-        mine = mine + ring[i]
-    full[me] = mine
+    mine = added([ring[i] for i in range(FAR)])
+    full[me] = mine.astype(BF16)
     gather = [
         remote(full.at[me], full.at[me], s_ag.at[i], r_ag.at[i], device) for i, (_, device) in enumerate(team)
     ]
@@ -466,14 +483,13 @@
         remote(full.at[senders[i]], full.at[senders[i]], s_ag.at[i], r_ag.at[i], device).wait_recv()
     for i, (device, src) in enumerate(wide_team):
         remote(norms.at[src], norms.at[src], s_norm.at[i], r_norm.at[i], device).wait_recv()
-    total = norms[0]
-    for i in range(1, NX * TEAM):
-        total = total + norms[i]
+    total = added([norms[i] for i in range(NX * TEAM)])
     scale = 1.0 / jnp.maximum(1.0, jnp.sqrt(total) / CLIP)
     for j in range(cols):
         for s in range(3):
-            gfeat_ref[s, :, pl.ds(j * LANES, LANES)] = scale * full[2 * j + s // 2, pl.ds((s % 2) * 8, TAPS), :]
-        gfilt_ref[pl.ds(j * per_col, per_col), :] = scale * full[2 * j + 1, pl.ds(8, per_col), :]
+            part = full[2 * j + s // 2].astype(F32)[(s % 2) * 8 : (s % 2) * 8 + TAPS]
+            gfeat_ref[s, :, pl.ds(j * LANES, LANES)] = scale * part
+        gfilt_ref[pl.ds(j * per_col, per_col), :] = scale * full[2 * j + 1].astype(F32)[8:]
 
     @pl.loop(0, cols)
     def _(j):
@@ -541,14 +557,13 @@
             pltpu.VMEM((cols, LAGS + rows, LANES), BF16),
             pltpu.VMEM((3, cols, rows + 8, LANES), F32),
             pltpu.VMEM((2, groups * BLOCK, LANES), F32),
-            pltpu.VMEM((cols, LANES, 2 * LANES), BF16),
-            pltpu.VMEM((cols, LANES, 2 * LANES), BF16),
-            pltpu.VMEM((cols, LANES, 2 * LANES), F32),
-            pltpu.VMEM((cols, 3 * TAPS, 8, LANES), F32),
-            pltpu.VMEM((TEAM, 16, LANES), F32),
-            pltpu.VMEM((TEAM - 1, 16, LANES), F32),
-            pltpu.VMEM((FAR, 16, LANES), F32),
-            pltpu.VMEM((TEAM, 16, LANES), F32),
+            pltpu.VMEM((cols, STACK, 2 * LANES), BF16),
+            pltpu.VMEM((cols, STACK, 2 * LANES), BF16),
+            pltpu.VMEM((cols * 24 * 8, LANES), F32),
+            pltpu.VMEM((TEAM, 16, LANES), BF16),
+            pltpu.VMEM((TEAM - 1, 16, LANES), BF16),
+            pltpu.VMEM((FAR, 16, LANES), BF16),
+            pltpu.VMEM((TEAM, 16, LANES), BF16),
             pltpu.VMEM((NX * TEAM, 1, LANES), F32),
             dma((6,)),
             dma((3,)),

time: 49.6 us -> 48.1 us (0.970)
  Pallas kernels: 48.7 us -> 47.2 us
    pallas_call x1, Pallas kernels: 46.4 us -> 44.9 us  [local(): pl.pallas_call(kernel, out_shape=shapes, in_specs=[hbm] * 6, out_specs=(h...]
where the time goes in v4:
time: 48.1 us; the launch traced here: 47.9 us
  Pallas kernels  47.2 us (98%)
  between operations  0.64 us (1%)
    pallas_call x1, Pallas kernels, local(): pl.pallas_call(kernel, out_shape=shapes, in_specs=[hbm] * 6, out_specs=(h...  44.9 us
    pallas_call x1, Pallas kernels, local(): pl.pallas_call(emit, out_shape=shapes, in_specs=[hbm] * 5, out_specs=(hbm...  2.29 us

profile of v4, /device:TPU:1, one launch (start us, length us, event | category | flops | bytes accessed | tf_op | source)
XLA Modules:
  0.0 47.9 jit_solution(18153106583463420798)
XLA Ops:
  0.6 44.9 %shard_map.101 = (bf16[256,1024]{1,0:T(8,128)(2,1)}, bf16[256,1024]{1,0:T(8,128)(2,1)}, bf16[256,1024]{1,0:T(8,128)(2,1)}, f32[3,7,1024]{2,1,0:T(8,128)}, f32[64,128]{1,0:T(8,128)}) custom-call(bf16[256,1024]{1,0:T(8,128)(2,1)} %bitcast.7, bf16[256,1024]{1,0:T(8,128)(2,1)} %bitcast.8, bf16[256,1024]{1,0:T(8,128)(2,1)} %bitcast.9, ...), custom_call_target="tpu_custom_call" | custom-call | flops 805306368 | bytes 3670016 | tf_op jit(solution)/shard_map/pallas_call | solution.py:536
  45.6 2.3 %shard_map.102 = (bf16[256,1024]{1,0:T(8,128)(2,1)}, bf16[256,1024]{1,0:T(8,128)(2,1)}, bf16[256,1024]{1,0:T(8,128)(2,1)}, f32[3,7,1024]{2,1,0:T(8,128)}, f32[64,128]{1,0:T(8,128)}) custom-call(bf16[256,1024]{1,0:T(8,128)(2,1)} %get-tuple-element.15.refs_0_, bf16[256,1024]{1,0:T(8,128)(2,1)} %get-tuple-element.16.refs_1_, ...), custom_call_target="tpu_custom_call" | custom-call | tf_op jit(solution)/shard_map/pallas_call | solution.py:597

commit v5 on v4

--- a/solution.py
+++ b/solution.py
@@ -74,6 +74,7 @@
     ring,
     full,
     norms,
+    own_norm,
     s_in,
     s_tail,
     r_tail,
@@ -131,10 +132,12 @@
     wide_team = []
     for dx in range(NX):
         for dy, dz, dc in steps:
-            if dx or dy or dz or dc:
+            if dx:
                 device = member(dy, dz, dc, lax.rem(tp + dx, NX))[1]
                 index = member((NY - dy) % NY, dz, dc, tp)[0]
-                wide_team.append((device, lax.rem(tp + NX - dx, NX) * TEAM + index))
+                hops = min(dx, NX - dx) + min(dy, NY - dy) + dz
+                wide_team.append((hops, device, lax.rem(tp + NX - dx, NX) * TEAM + index))
+    wide_team = [entry[1:] for entry in sorted(wide_team, key=lambda entry: -entry[0])]
     far = [at(tp, yi, lax.rem(z_far + d, FAR) * 2 + z_low, core) for d in range(1, FAR)]
 
     barrier = pltpu.get_barrier_semaphore()
@@ -197,7 +200,62 @@
     low_spans = [(HALO, CHUNK - HALO), (CHUNK, CHUNK)]
     high_spans = [(half, CHUNK), (half + CHUNK, CHUNK)]
 
-    loads[0].wait()
+    for copy in loads[:4]:
+        copy.wait()
+
+    @pl.loop(0, cols)
+    def _(j):
+        widen(1, j, k_ref)
+        widen(2, j, v_ref)
+        products(j, high_spans)
+
+    for copy in loads[4:]:
+        copy.wait()
+
+    pl.semaphore_wait(barrier, len(greeted))
+
+    for peer in x_peers + z_two:
+        pl.semaphore_signal(hear.at[0], inc=1, device_id=peer, device_id_type=MESH)
+
+    tails = [
+        remote(ref.at[pl.ds(rows - HALO, HALO), :], tail.at[s], s_tail.at[s], r_tail.at[s], after)
+        for s, ref in enumerate((q_ref, k_ref, v_ref))
+    ]
+    aheads = [
+        remote(ref.at[pl.ds(0, HALO), :], ahead_raw.at[i], s_ahead.at[i], r_ahead.at[i], before)
+        for i, ref in enumerate((q_ref, cot_ref))
+    ]
+    for copy in tails + aheads:
+        copy.start()
+
+    def prod_copy(j):
+        return remote(
+            prod.at[j, pl.ds(rows, LAGS), :], prod.at[j, pl.ds(0, LAGS), :], s_prod.at[j], r_prod.at[j], after
+        )
+
+    def mid_copy(j):
+        return remote(
+            mid.at[j, pl.ds(HALO, LAGS - HALO), :],
+            mid.at[j, pl.ds(rows + HALO, LAGS - HALO), :],
+            s_mid.at[j],
+            r_mid.at[j],
+            before,
+        )
+
+    @pl.loop(0, cols)
+    def _(j):
+        prod_copy(j).start()
+
+    @pl.loop(0, cols)
+    def _(j):
+        widen(0, j, q_ref)
+        mids(j, low_spans)
+        mid_copy(j).start()
+
+    @pl.loop(0, cols)
+    def _(j):
+        mids(j, high_spans)
+        products(j, low_spans)
 
     lag_row = lax.broadcasted_iota(jnp.int32, (LAGS, 2 * LANES), 0)
     lag_col = lax.broadcasted_iota(jnp.int32, (LAGS, 2 * LANES), 1)
@@ -212,63 +270,6 @@
         for j in range(cols):
             span = pl.ds(j * STACK, STACK)
             table[j] = jnp.concatenate([tabs[0, span, :], tabs[1, span, :]], axis=1).astype(BF16)
-
-    for copy in loads[1:4]:
-        copy.wait()
-
-    @pl.loop(0, cols)
-    def _(j):
-        widen(1, j, k_ref)
-        widen(2, j, v_ref)
-        products(j, high_spans)
-
-    for copy in loads[4:]:
-        copy.wait()
-
-    pl.semaphore_wait(barrier, len(greeted))
-
-    for peer in x_peers + z_two:
-        pl.semaphore_signal(hear.at[0], inc=1, device_id=peer, device_id_type=MESH)
-
-    tails = [
-        remote(ref.at[pl.ds(rows - HALO, HALO), :], tail.at[s], s_tail.at[s], r_tail.at[s], after)
-        for s, ref in enumerate((q_ref, k_ref, v_ref))
-    ]
-    aheads = [
-        remote(ref.at[pl.ds(0, HALO), :], ahead_raw.at[i], s_ahead.at[i], r_ahead.at[i], before)
-        for i, ref in enumerate((q_ref, cot_ref))
-    ]
-    for copy in tails + aheads:
-        copy.start()
-
-    def prod_copy(j):
-        return remote(
-            prod.at[j, pl.ds(rows, LAGS), :], prod.at[j, pl.ds(0, LAGS), :], s_prod.at[j], r_prod.at[j], after
-        )
-
-    def mid_copy(j):
-        return remote(
-            mid.at[j, pl.ds(HALO, LAGS - HALO), :],
-            mid.at[j, pl.ds(rows + HALO, LAGS - HALO), :],
-            s_mid.at[j],
-            r_mid.at[j],
-            before,
-        )
-
-    @pl.loop(0, cols)
-    def _(j):
-        prod_copy(j).start()
-
-    @pl.loop(0, cols)
-    def _(j):
-        widen(0, j, q_ref)
-        mids(j, low_spans)
-        mid_copy(j).start()
-
-    @pl.loop(0, cols)
-    def _(j):
-        mids(j, high_spans)
-        products(j, low_spans)
 
     for copy in tails + aheads:
         copy.wait_recv()
@@ -356,7 +357,7 @@
     def tile_rows(j):
         return pl.ds(pl.multiple_of(j * STACK, STACK), STACK)
 
-    @pl.loop(0, cols, unroll=4)
+    @pl.loop(0, cols)
     def _(j):
         acc = forward(j, half)
         more, pairs = backward(j, 0)
@@ -371,7 +372,7 @@
     for peer in z_four:
         pl.semaphore_signal(hear.at[1], inc=1, device_id=peer, device_id_type=MESH)
 
-    @pl.loop(0, cols, unroll=4)
+    @pl.loop(0, cols)
     def _(j):
         prod_copy(j).wait_recv()
         mid_copy(j).wait_recv()
@@ -465,22 +466,27 @@
         remote(ring.at[src], ring.at[src], s_far.at[i], r_far.at[i], device).wait_recv()
     mine = added([ring[i] for i in range(FAR)])
     full[me] = mine.astype(BF16)
+
+    def squares(index):
+        value = full[index].astype(F32)
+        total = jnp.sum(jnp.sum(value * value, axis=0, keepdims=True), axis=1, keepdims=True)
+        return jnp.broadcast_to(total, (1, LANES))
+
+    seat = tp * TEAM + me
+    own_norm[...] = squares(me)
+    tell = [
+        remote(own_norm, norms.at[seat], s_norm.at[i], r_norm.at[i], device)
+        for i, (device, _) in enumerate(wide_team)
+    ]
     gather = [
         remote(full.at[me], full.at[me], s_ag.at[i], r_ag.at[i], device) for i, (_, device) in enumerate(team)
     ]
-    for copy in gather:
-        copy.start()
-    squares = jnp.sum(jnp.sum(mine * mine, axis=0, keepdims=True), axis=1, keepdims=True)
-    seat = tp * TEAM + me
-    norms[seat] = jnp.broadcast_to(squares, (1, LANES))
-    tell = [
-        remote(norms.at[seat], norms.at[seat], s_norm.at[i], r_norm.at[i], device)
-        for i, (device, _) in enumerate(wide_team)
-    ]
-    for copy in tell:
+    for copy in tell + gather:
         copy.start()
     for i, (_, device) in enumerate(team):
         remote(full.at[senders[i]], full.at[senders[i]], s_ag.at[i], r_ag.at[i], device).wait_recv()
+    for index in range(TEAM):
+        norms[tp * TEAM + index] = squares(index)
     for i, (device, src) in enumerate(wide_team):
         remote(norms.at[src], norms.at[src], s_norm.at[i], r_norm.at[i], device).wait_recv()
     total = added([norms[i] for i in range(NX * TEAM)])
@@ -565,6 +571,7 @@
             pltpu.VMEM((FAR, 16, LANES), BF16),
             pltpu.VMEM((TEAM, 16, LANES), BF16),
             pltpu.VMEM((NX * TEAM, 1, LANES), F32),
+            pltpu.VMEM((1, LANES), F32),
             dma((6,)),
             dma((3,)),
             dma((3,)),
@@ -582,8 +589,8 @@
             dma((FAR - 1,)),
             dma((TEAM - 1,)),
             dma((TEAM - 1,)),
-            dma((NX * TEAM - 1,)),
-            dma((NX * TEAM - 1,)),
+            dma(((NX - 1) * TEAM,)),
+            dma(((NX - 1) * TEAM,)),
             dma((3,)),
             pltpu.SemaphoreType.REGULAR((2,)),
         ],

time: 48.1 us -> 47.3 us (0.983)
  Pallas kernels: 47.2 us -> 46.4 us
    pallas_call x1, Pallas kernels: 44.9 us -> 44.1 us  [local(): pl.pallas_call(kernel, out_shape=shapes, in_specs=[hbm] * 6, out_specs=(h...]
where the time goes in v5:
time: 47.3 us; the launch traced here: 47.1 us
  Pallas kernels  46.4 us (98%)
  between operations  0.64 us (1%)
    pallas_call x1, Pallas kernels, local(): pl.pallas_call(kernel, out_shape=shapes, in_specs=[hbm] * 6, out_specs=(h...  44.1 us
    pallas_call x1, Pallas kernels, local(): pl.pallas_call(emit, out_shape=shapes, in_specs=[hbm] * 5, out_specs=(hbm...  2.29 us

profile of v5, /device:TPU:1, one launch (start us, length us, event | category | flops | bytes accessed | tf_op | source)
XLA Modules:
  0.0 47.1 jit_solution(2710109926551706457)
XLA Ops:
  0.6 44.1 %shard_map.101 = (bf16[256,1024]{1,0:T(8,128)(2,1)}, bf16[256,1024]{1,0:T(8,128)(2,1)}, bf16[256,1024]{1,0:T(8,128)(2,1)}, f32[3,7,1024]{2,1,0:T(8,128)}, f32[64,128]{1,0:T(8,128)}) custom-call(bf16[256,1024]{1,0:T(8,128)(2,1)} %bitcast.7, bf16[256,1024]{1,0:T(8,128)(2,1)} %bitcast.8, bf16[256,1024]{1,0:T(8,128)(2,1)} %bitcast.9, ...), custom_call_target="tpu_custom_call" | custom-call | flops 805306368 | bytes 3670016 | tf_op jit(solution)/shard_map/pallas_call | solution.py:542
  44.8 2.3 %shard_map.102 = (bf16[256,1024]{1,0:T(8,128)(2,1)}, bf16[256,1024]{1,0:T(8,128)(2,1)}, bf16[256,1024]{1,0:T(8,128)(2,1)}, f32[3,7,1024]{2,1,0:T(8,128)}, f32[64,128]{1,0:T(8,128)}) custom-call(bf16[256,1024]{1,0:T(8,128)(2,1)} %get-tuple-element.15.refs_0_, bf16[256,1024]{1,0:T(8,128)(2,1)} %get-tuple-element.16.refs_1_, ...), custom_call_target="tpu_custom_call" | custom-call | tf_op jit(solution)/shard_map/pallas_call | solution.py:604

commit v6 on v5

--- a/solution.py
+++ b/solution.py
@@ -402,10 +402,10 @@
         high = tabs[1, pl.ds(b, groups, stride=BLOCK), :]
         lags = lags + pltpu.roll(jnp.where(lane >= b, low, high), LANES - b, 1)
     for j in range(cols):
-        pay[2 * j] = taps_total[j * 24 : j * 24 + 16].astype(BF16)
+        pay[2 * j] = taps_total[j * 24 : j * 24 + 16]
         pay[2 * j + 1] = jnp.concatenate(
             [taps_total[j * 24 + 16 : j * 24 + 24], lags[j * per_col : (j + 1) * per_col]], axis=0
-        ).astype(BF16)
+        )
 
     scatter = [
         remote(pay.at[index], got.at[i], s_rs.at[i], r_rs.at[i], device)
@@ -437,7 +437,7 @@
     for copy in scatter:
         copy.wait_recv()
     mine = added([pay[me]] + [got[i] for i in range(len(team))])
-    ring[z_far] = mine.astype(BF16)
+    ring[z_far] = mine
     spread_far = [
         remote(ring.at[z_far], ring.at[z_far], s_far.at[i], r_far.at[i], device)
         for i, device in enumerate(far)
@@ -465,7 +465,7 @@
         src = lax.rem(z_far + FAR - 1 - i, FAR)
         remote(ring.at[src], ring.at[src], s_far.at[i], r_far.at[i], device).wait_recv()
     mine = added([ring[i] for i in range(FAR)])
-    full[me] = mine.astype(BF16)
+    full[me] = mine
 
     def squares(index):
         value = full[index].astype(F32)
@@ -566,10 +566,10 @@
             pltpu.VMEM((cols, STACK, 2 * LANES), BF16),
             pltpu.VMEM((cols, STACK, 2 * LANES), BF16),
             pltpu.VMEM((cols * 24 * 8, LANES), F32),
-            pltpu.VMEM((TEAM, 16, LANES), BF16),
-            pltpu.VMEM((TEAM - 1, 16, LANES), BF16),
-            pltpu.VMEM((FAR, 16, LANES), BF16),
-            pltpu.VMEM((TEAM, 16, LANES), BF16),
+            pltpu.VMEM((TEAM, 16, LANES), F32),
+            pltpu.VMEM((TEAM - 1, 16, LANES), F32),
+            pltpu.VMEM((FAR, 16, LANES), F32),
+            pltpu.VMEM((TEAM, 16, LANES), F32),
             pltpu.VMEM((NX * TEAM, 1, LANES), F32),
             pltpu.VMEM((1, LANES), F32),
             dma((6,)),

time: 47.3 us -> 48.6 us (1.027)
  Pallas kernels: 46.4 us -> 47.8 us
    pallas_call x1, Pallas kernels: 44.1 us -> 45.5 us  [local(): pl.pallas_call(kernel, out_shape=shapes, in_specs=[hbm] * 6, out_specs=(h...]
where the time goes in v6:
time: 48.6 us; the launch traced here: 48.4 us
  Pallas kernels  47.8 us (98%)
  between operations  0.64 us (1%)
    pallas_call x1, Pallas kernels, local(): pl.pallas_call(kernel, out_shape=shapes, in_specs=[hbm] * 6, out_specs=(h...  45.5 us
    pallas_call x1, Pallas kernels, local(): pl.pallas_call(emit, out_shape=shapes, in_specs=[hbm] * 5, out_specs=(hbm...  2.29 us

profile of v6, /device:TPU:1, one launch (start us, length us, event | category | flops | bytes accessed | tf_op | source)
XLA Modules:
  0.0 48.4 jit_solution(15653330028679741245)
XLA Ops:
  0.6 45.5 %shard_map.101 = (bf16[256,1024]{1,0:T(8,128)(2,1)}, bf16[256,1024]{1,0:T(8,128)(2,1)}, bf16[256,1024]{1,0:T(8,128)(2,1)}, f32[3,7,1024]{2,1,0:T(8,128)}, f32[64,128]{1,0:T(8,128)}) custom-call(bf16[256,1024]{1,0:T(8,128)(2,1)} %bitcast.7, bf16[256,1024]{1,0:T(8,128)(2,1)} %bitcast.8, bf16[256,1024]{1,0:T(8,128)(2,1)} %bitcast.9, ...), custom_call_target="tpu_custom_call" | custom-call | flops 805306368 | bytes 3670016 | tf_op jit(solution)/shard_map/pallas_call | solution.py:542
  46.1 2.3 %shard_map.102 = (bf16[256,1024]{1,0:T(8,128)(2,1)}, bf16[256,1024]{1,0:T(8,128)(2,1)}, bf16[256,1024]{1,0:T(8,128)(2,1)}, f32[3,7,1024]{2,1,0:T(8,128)}, f32[64,128]{1,0:T(8,128)}) custom-call(bf16[256,1024]{1,0:T(8,128)(2,1)} %get-tuple-element.15.refs_0_, bf16[256,1024]{1,0:T(8,128)(2,1)} %get-tuple-element.16.refs_1_, ...), custom_call_target="tpu_custom_call" | custom-call | tf_op jit(solution)/shard_map/pallas_call | solution.py:604
